TPU v7x, 32 devices: a whole 2x2x4 slice. The times are simulated.
32 devices in a mesh: seq: 2 (over core), shard: 16 (over z, y, x).
Axes of the slice: x: 2, y: 2, z: 4, core: 2. Of those that a mesh axis runs over, the one named last changes fastest.
Arguments:
- tokens: bfloat16 [16, 8, 392, 512], P('shard', 'seq'), may hold values from -26 to 26
- norm1_gain: bfloat16 [512], P('shard'), may hold values from 0.099609375 to 1.8984375
- norm1_bias: bfloat16 [512], P('shard'), may hold values from -1.75 to 1.75
- qkv_weight: bfloat16 [512, 1536], P('shard'), may hold values from -0.25 to 0.25
- qv_bias: bfloat16 [1024], P('shard'), may hold values from -1.75 to 1.75
- position_table: bfloat16 [2535, 16], replicated, may hold values from -4 to 4
- proj_weight: bfloat16 [512, 512], P(None, 'shard'), may hold values from -1.5 to 1.5
- proj_bias: bfloat16 [512], P('shard'), may hold values from -1.75 to 1.75
- norm2_gain: bfloat16 [512], P('shard'), may hold values from 0.099609375 to 1.8984375
- norm2_bias: bfloat16 [512], P('shard'), may hold values from -1.75 to 1.75
- fc1_weight: bfloat16 [512, 2048], P('shard'), may hold values from -0.25 to 0.25
- fc1_bias: bfloat16 [2048], P('shard'), may hold values from -3 to 3
- fc2_weight: bfloat16 [2048, 512], P(None, 'shard'), may hold values from -0.125 to 0.125
- fc2_bias: bfloat16 [512], P('shard'), may hold values from -1.75 to 1.75
- rel_index: int32 [392, 392], replicated, may hold values from 0 to 2534, as said below
- region_ids: int32 [8, 392], P('seq'), may hold values from 0 to 26, as said below
- cotangent: bfloat16 [16, 8, 392, 512], P('shard', 'seq'), may hold values from -8 to 8
Outputs:
- block_out: bfloat16 [16, 8, 392, 512], P('shard', 'seq')
- input_grad: float32 [16, 8, 392, 512], P('shard', 'seq')
- norm1_gain_grad: float32 [512], P('shard')
- norm1_bias_grad: float32 [512], P('shard')
- qkv_weight_grad: float32 [512, 1536], P('shard')
- qv_bias_grad: float32 [1024], P('shard')
- position_table_grad: float32 [2535, 16], replicated
- proj_weight_grad: float32 [512, 512], P(None, 'shard')
- proj_bias_grad: float32 [512], P('shard')
- norm2_gain_grad: float32 [512], P('shard')
- norm2_bias_grad: float32 [512], P('shard')
- fc1_weight_grad: float32 [512, 2048], P('shard')
- fc1_bias_grad: float32 [2048], P('shard')
- fc2_weight_grad: float32 [2048, 512], P(None, 'shard')
- fc2_bias_grad: float32 [512], P('shard')
Inputs may be any that keep to these rules, and one draw needn't show every extreme that they name: `rel_index`: each relative offset of the two positions of a pair has a row of its own, relabelled anew in each draw; every row is used. `region_ids`: 9 a + 3 b + c with labels a, b, c that never fall along time, height and width of the shifted grid, each of the labels 0, 1, 2 occurring along each.
All inputs are finite; a program needn't handle non-finite values.
Results may differ from a plain program's by a relative error of at most 0.02.
Values may be sent and summed in bfloat16 or wider, within the bound.
No kernel may reach another device: no remote copies, remote signals or barrier semaphores. Data moves between devices by JAX's collectives and lax.ppermute only.
A program may use at most 448 MiB of HBM per device.

v0:
```python
import functools

import jax
import jax.numpy as jnp
import numpy as np
from jax import lax
from jax.experimental import pallas as pl
from jax.experimental.pallas import tpu as pltpu
from jax.sharding import PartitionSpec as P

HEADS = 16
HEAD_DIM = 32
WT = 8
WH = 7
WW = 7
WIN_TOK = WT * WH * WW
EPS = 1e-05

BF=jnp.bfloat16; F32=jnp.float32
LOG2E=1.4426950408889634; LN2=0.6931471805599453
SCALE=HEAD_DIM**-0.5
BIG=-(2.0**30)
GROUP=4
VM=56*1024*1024

def cost(micros):
    return pl.CostEstimate(flops=int(micros * 1e9), bytes_accessed=int(micros * 3.6e6), transcendentals=0)


def nt(a,b): return lax.dot_general(a,b,(((1,),(1,)),((),())),preferred_element_type=F32)
def nn(a,b): return jnp.dot(a,b,preferred_element_type=F32)

def placed(block, at, rows):
    parts=[]
    if at: parts.append(jnp.zeros((at,block.shape[1]),block.dtype))
    parts.append(block)
    if rows-at-block.shape[0]: parts.append(jnp.zeros((rows-at-block.shape[0],block.shape[1]),block.dtype))
    return jnp.concatenate(parts,axis=0)

PAIR = 2 * GROUP
SAFE = 2.0**60


def attend_kernel(
    q_ref, k_ref, v_ref, bias_ref, mq_ref, mk_ref, ctx_ref, ctx_tok_ref, e_ref, r_ref, scores
):
    n = q_ref.shape[2]
    ones = jnp.ones((16, n), BF)
    mask_rows = placed(mq_ref[0], 0, 128)
    lhs = [jnp.concatenate([k_ref[0, :, 128 * g : 128 * (g + 1)], mk_ref[0]], axis=1) for g in range(2)]
    rows = lambda h: slice(h * HEAD_DIM, (h + 1) * HEAD_DIM)

    def score(h):
        rhs = jnp.concatenate([placed(q_ref[0, rows(h), :], h % GROUP * HEAD_DIM, 128), mask_rows], axis=0)
        scores[h % 2] = nn(lhs[h // GROUP], rhs)

    def context(h):
        c = nn(jnp.concatenate([v_ref[0, rows(h), :], ones], axis=0), e_ref[0, h])
        total = c[HEAD_DIM : HEAD_DIM + 1]
        r = 1.0 / total
        ctx_ref[0, rows(h), :] = (c[:HEAD_DIM] * r).astype(BF)
        r_ref[0, h : h + 1, :] = r
        return total

    totals = []
    score(0)
    for h in range(PAIR):
        if h + 1 < PAIR:
            score(h + 1)
        e_ref[0, h] = jnp.exp(scores[h % 2] + bias_ref[h].astype(F32)).astype(BF)
        if h:
            totals.append(context(h - 1))
    totals.append(context(PAIR - 1))
    every = jnp.concatenate(totals, axis=0)
    ordinary = jnp.logical_and(jnp.min(every) > 1.0 / SAFE, jnp.max(every) < SAFE)

    @pl.when(jnp.logical_not(ordinary))
    def _():
        spot = lax.broadcasted_iota(jnp.int32, (128, n), 0) // HEAD_DIM

        def again(h, carry):
            at = pl.ds(pl.multiple_of(h * HEAD_DIM, HEAD_DIM), HEAD_DIM)
            group = pl.ds(pl.multiple_of(h // GROUP * 128, 128), 128)
            q = jnp.concatenate([q_ref[0, at, :].astype(F32)] * GROUP, axis=0)
            rhs = jnp.where(spot == h % GROUP, q, 0.0).astype(BF)
            s = nn(jnp.concatenate([k_ref[0, :, group], mk_ref[0]], axis=1), jnp.concatenate([rhs, mask_rows], axis=0))
            s = s + bias_ref[h].astype(F32)
            e = jnp.exp(s - jnp.max(s, axis=0, keepdims=True)).astype(BF)
            e_ref[0, h] = e
            c = nn(jnp.concatenate([v_ref[0, at, :], ones], axis=0), e)
            r = 1.0 / c[HEAD_DIM : HEAD_DIM + 1]
            ctx_ref[0, at, :] = (c[:HEAD_DIM] * r).astype(BF)
            r_ref[0, pl.ds(h, 1), :] = r
            return carry

        lax.fori_loop(0, PAIR, again, 0)

    ctx_tok_ref[0] = jnp.transpose(ctx_ref[0])


def attend(side,qT,k,vT,bias,mq,mk):
    nw,width,n=qT.shape
    half=width//2
    wins=mk.shape[0]
    return pl.pallas_call(
        attend_kernel,
        grid=(nw,),
        in_specs=[
            pl.BlockSpec((1,half,n),lambda w:(w,side,0)),
            pl.BlockSpec((1,n,half),lambda w:(w,0,side)),
            pl.BlockSpec((1,half,n),lambda w:(w,side,0)),
            pl.BlockSpec((PAIR,n,n),lambda w:(0,0,0)),
            pl.BlockSpec((1,32,n),lambda w:(w%wins,0,0)),
            pl.BlockSpec((1,n,128),lambda w:(w%wins,0,0)),
        ],
        out_specs=[
            pl.BlockSpec((1,half,n),lambda w:(w,0,0)),
            pl.BlockSpec((1,n,half),lambda w:(w,0,0)),
            pl.BlockSpec((1,PAIR,n,n),lambda w:(w,0,0,0)),
            pl.BlockSpec((1,PAIR,n),lambda w:(w,0,0)),
        ],
        out_shape=[
            jax.ShapeDtypeStruct((nw,half,n),BF),
            jax.ShapeDtypeStruct((nw,n,half),BF),
            jax.ShapeDtypeStruct((nw,PAIR,n,n),BF),
            jax.ShapeDtypeStruct((nw,PAIR,n),F32),
        ],
        scratch_shapes=[pltpu.VMEM((2,n,n),F32)],
        compiler_params=pltpu.CompilerParams(vmem_limit_bytes=VM),
        name="attend", cost_estimate=cost(10),
    )(qT,k,vT,bias,mq,mk)

SPREAD=768
FLAT=1408
WIDE=2816

def spread_ones():
    n=WT*WH*WW
    tok=np.arange(n); c=tok//(WW*WT); e=tok//WT%WW; a=tok%WT
    out=np.zeros((n,SPREAD),np.float32); out[tok,c*104+e*8+a]=1
    return out

def lane16(mirror):
    out=np.zeros((128,256),np.float32)
    for u in range(16):
        for a in range(8):
            out[u*8+a,u*16+(7-a if mirror else a)]=1
    return out

def back_kernel(
    e_ref, k_ref, v_ref, q_ref, g_ref, ctx_ref, r_ref, sp_ref, l16_ref, dq_ref, dk_ref, dv_ref, tab_ref, tot, acc, prob, low
):
    w = pl.program_id(1)
    nw = pl.num_programs(1)
    first = pl.program_id(0) * GROUP
    n = q_ref.shape[2]
    rows = lambda h: slice(h * HEAD_DIM, (h + 1) * HEAD_DIM)

    @pl.when(w == 0)
    def _():
        tot[...] = jnp.zeros_like(tot)

    grads, inner = [], []
    for h in range(GROUP):
        go = g_ref[0, rows(h), :].astype(F32) * r_ref[0, pl.ds(first + h, 1), :]
        inner.append(jnp.sum(go * ctx_ref[0, rows(h), :].astype(F32), axis=0, keepdims=True))
        grads.append(placed(go.astype(BF), h * HEAD_DIM, 128))

    def prob_grad(h):
        prob[h % 2] = nn(v_ref[0], grads[h])

    dq, dk, dv = [], [], []

    def score_side(h):
        dk.append(nt(low[h % 2], placed(q_ref[0, rows(h), :], h * HEAD_DIM, 128)))
        dq.append(nn(k_ref[0, rows(h), :], low[h % 2]) * SCALE)

    def fold(h):
        x = nn(tot[h].astype(BF), sp_ref[...])
        full = jnp.zeros((8, FLAT), F32)
        for d in range(WH):
            part = jnp.zeros((8, SPREAD), F32)
            for f in range(WW):
                j = (d * WW + f) * 8
                part = part + (pltpu.roll(x[j : j + 8, :], 8 * (WW - 1 - f), 1) if f < WW - 1 else x[j : j + 8, :])
            broad = jnp.concatenate([part, jnp.zeros((8, FLAT - SPREAD), F32)], axis=1)
            full = full + (pltpu.roll(broad, 104 * (WH - 1 - d), 1) if d < WH - 1 else broad)
        acc[h * 8 : (h + 1) * 8, :] = full

    def sweep(last):
        prob_grad(0)
        for h in range(GROUP):
            ds = e_ref[0, h].astype(F32) * (prob[h % 2] - inner[h])
            low[h % 2] = ds.astype(BF)
            tot[h] += ds
            dv.append(nt(e_ref[0, h], grads[h]))
            if h + 1 < GROUP:
                prob_grad(h + 1)
            score_side(h)
            if last:
                fold(h)
        dq_ref[0] = jnp.transpose(jnp.concatenate(dq, axis=0).astype(BF))
        dv_ref[0] = ((dv[0] + dv[1]) + (dv[2] + dv[3])).astype(BF)
        dk_ref[0] = ((dk[0] + dk[1]) + (dk[2] + dk[3])).astype(BF)
        dq.clear()
        dk.clear()
        dv.clear()

    @pl.when(w < nw - 1)
    def _():
        sweep(False)

    @pl.when(w == nw - 1)
    def _():
        sweep(True)
        a = acc[...]
        hi = a.astype(BF)
        rest = (a - hi.astype(F32)).astype(BF)
        wide = []
        for t in range(FLAT // 128):
            c = slice(t * 128, (t + 1) * 128)
            wide.append(nn(hi[:, c], l16_ref[...]) + nn(rest[:, c], l16_ref[...]))
        y = jnp.concatenate(wide, axis=1)
        for h in range(GROUP):
            z = pltpu.roll(y[h * 8 : (h + 1) * 8, :], 0, 1, stride=1, stride_axis=0)
            tab_ref[0, h : h + 1, :] = jnp.sum(z, axis=0, keepdims=True)


def attend_back(side,e,kT,v,qT,gT,ctxT,r,sp,l16):
    nw,width,n=qT.shape
    feat=pl.BlockSpec((1,128,n),lambda g,w:(w,2*side+g,0))
    tok=pl.BlockSpec((1,n,128),lambda g,w:(w,0,2*side+g))
    own=pl.BlockSpec((1,n,128),lambda g,w:(w,0,g))
    return pl.pallas_call(
        back_kernel,
        grid=(2,nw),
        in_specs=[
            pl.BlockSpec((1,GROUP,n,n),lambda g,w:(w,g,0,0)),
            feat,tok,feat,feat,pl.BlockSpec((1,128,n),lambda g,w:(w,g,0)),
            pl.BlockSpec((1,PAIR,n),lambda g,w:(w,0,0)),
            pl.BlockSpec(sp.shape,lambda g,w:(0,0)),
            pl.BlockSpec(l16.shape,lambda g,w:(0,0)),
        ],
        out_specs=[own,own,own,pl.BlockSpec((1,GROUP,WIDE),lambda g,w:(g,0,0))],
        out_shape=[
            jax.ShapeDtypeStruct((nw,n,256),BF),
            jax.ShapeDtypeStruct((nw,n,256),BF),
            jax.ShapeDtypeStruct((nw,n,256),BF),
            jax.ShapeDtypeStruct((2,GROUP,WIDE),F32),
        ],
        scratch_shapes=[
            pltpu.VMEM((GROUP,n,n),F32),pltpu.VMEM((GROUP*8,FLAT),F32),pltpu.VMEM((2,n,n),F32),pltpu.VMEM((2,n,n),BF),
        ],
        compiler_params=pltpu.CompilerParams(vmem_limit_bytes=VM),
        name="attend_back", cost_estimate=cost(20),
    )(e,kT,v,qT,gT,ctxT,r,sp,l16)

def lane_maps(mirror):
    lane=np.arange(WIDE); pq=lane//16; o=lane%16
    p=pq//13; q=pq%13
    ok=(pq<169)&(o<15)
    if mirror: o=14-o
    A=o>=7; b=np.where(A,14-o,7-o); C=p>=6; d=np.where(C,12-p,6-p); E=q>=6; f=np.where(E,12-q,6-q)
    col=(b*WH+d)*WW+f
    corner=A*4+C*2+E*1
    return np.where(ok,col,-1).astype(np.int32), np.where(ok,corner,-1).astype(np.int32)

CORNER_ROWS=[(a*WH+c)*WW+e for a in (0,WT-1) for c in (0,WH-1) for e in (0,WW-1)]

def prepare_kernel(rel_ref,maps_ref,table_ref,region_ref,order_ref,l8_ref,lab_ref,narrow_ref,mk_ref,mq_ref):
    values=[]
    n=rel_ref.shape[1]
    rel=jnp.concatenate([rel_ref[row:row+1,:] for row in CORNER_ROWS],axis=0)
    hi=(rel>>6).astype(F32).astype(BF); lo=(rel&63).astype(F32).astype(BF)
    both=jnp.concatenate([hi,lo],axis=0)
    corners=lax.broadcasted_iota(jnp.int32,(8,256),0)
    rows=lax.broadcasted_iota(jnp.int32,(n,256),0)
    trow=lax.broadcasted_iota(jnp.int32,(table_ref.shape[1],256),0)
    for t in range(WIDE//256):
        c=slice(t*256,(t+1)*256)
        for version in range(2):
            col=maps_ref[2*version:2*version+1,c]; cor=maps_ref[2*version+1:2*version+2,c]
            m=jnp.where(rows==col,1.0,0.0).astype(BF)
            y=nn(both,m)
            full=y[:8]*64.0+y[8:]
            lab=jnp.sum(jnp.where(corners==cor,full,0.0),axis=0,keepdims=True)
            lab=jnp.where(cor>=0,lab,-1.0).astype(jnp.int32)
            lab_ref[version:version+1,c]=lab
            if version==0:
                hot=jnp.where(trow==lab,1.0,0.0).astype(BF)
                values.append(nn(table_ref[...],hot))
    values=jnp.concatenate(values,axis=1)
    rolled=[]
    for h in range(HEADS):
        line=jnp.broadcast_to(values[h:h+1],(8,WIDE))
        rolled.append(pltpu.roll(line,WIDE-7,1,stride=1,stride_axis=0))
    rolled=jnp.concatenate(rolled,axis=0).astype(BF)
    for t in range(FLAT//128):
        narrow_ref[:,t*128:(t+1)*128]=nn(rolled[:,t*256:(t+1)*256],l8_ref[...])
    wins=region_ref.shape[0]
    region=jnp.concatenate([region_ref[...].astype(F32),jnp.zeros((16-wins,n),F32)],axis=0).astype(BF)
    across=nt(region,order_ref[...])
    down=nt(order_ref[...],region)
    lanes=lax.broadcasted_iota(jnp.int32,(n,128),1).astype(F32)
    subs=lax.broadcasted_iota(jnp.int32,(32,n),0).astype(F32)
    for w in range(wins):
        mk_ref[w]=jnp.where(down[:,w:w+1]==lanes,1.0,0.0).astype(BF)
        mq_ref[w]=jnp.where(across[w:w+1,:]==subs,0.0,BIG).astype(BF)

def prepare(rel_index,maps,table_t,region_ids,order,l8):
    wins,n=region_ids.shape
    return pl.pallas_call(
        prepare_kernel,
        out_shape=[
            jax.ShapeDtypeStruct((2,WIDE),jnp.int32),
            jax.ShapeDtypeStruct((HEADS*8,FLAT),F32),
            jax.ShapeDtypeStruct((wins,n,128),BF),
            jax.ShapeDtypeStruct((wins,32,n),BF),
        ],
        compiler_params=pltpu.CompilerParams(vmem_limit_bytes=VM),
        name="prepare", cost_estimate=cost(6),
    )(rel_index,maps,table_t,region_ids,order,l8)

def spread_spots():
    place = np.arange(WIN_TOK)
    lane = place // (WW * WT) * 104 + place // WT % WW * 8 + place % WT + 8 * (WW - 1)
    return np.broadcast_to(lane[:, None], (WIN_TOK, 128)).astype(np.int32)


def bias_kernel(narrow_ref, spot_ref, bias_ref, held):
    heads, n, _ = bias_ref.shape
    rows = []
    for h in range(heads):
        line = narrow_ref[8 * h : 8 * h + 8, :]
        for d in range(WH):
            rows.append((pltpu.roll(line, FLAT - 104 * (WH - 1 - d), 1) if d < WH - 1 else line)[:, :SPREAD])
    rows = jnp.concatenate(rows, axis=0).astype(BF)
    spots = jnp.concatenate([spot_ref[...]] * (SPREAD // 128), axis=1)
    lanes = lax.broadcasted_iota(jnp.int32, (n, SPREAD), 1)
    for f in range(WW):
        hot = jnp.where(lanes == spots - 8 * f, 1.0, 0.0).astype(BF)
        y = nt(rows, hot)
        for h in range(heads):
            for d in range(WH):
                at = (h * WH + d) * 8
                held[h, (d * WW + f) * 8 : (d * WW + f + 1) * 8, :] = y[at : at + 8, :]
    for h in range(heads):
        bias_ref[h] = held[h].astype(BF)


def bias_half(side, narrow, spots):
    n = spots.shape[0]
    heads = HEADS // 2
    return pl.pallas_call(
        bias_kernel,
        grid=(1,),
        in_specs=[pl.BlockSpec((8 * heads, FLAT), lambda i: (side, 0)), pl.BlockSpec(spots.shape, lambda i: (0, 0))],
        out_specs=pl.BlockSpec((heads, n, n), lambda i: (0, 0, 0)),
        out_shape=jax.ShapeDtypeStruct((heads, n, n), BF),
        scratch_shapes=[pltpu.VMEM((heads, n, n), F32)],
        compiler_params=pltpu.CompilerParams(vmem_limit_bytes=VM),
        name="position_bias", cost_estimate=cost(5),
    )(narrow, spots)


def spill_kernel(lab_ref,g_ref,out_ref):
    g=g_ref[...]
    hi=g.astype(BF); r1=g-hi.astype(F32); mid=r1.astype(BF); lo=(r1-mid.astype(F32)).astype(BF)
    three=jnp.concatenate([hi,mid,lo],axis=0)
    rows=out_ref.shape[1]
    trow=lax.broadcasted_iota(jnp.int32,(rows,256),0)
    tot=jnp.zeros((48,rows),F32)
    for t in range(WIDE//256):
        c=slice(t*256,(t+1)*256)
        hot=jnp.where(trow==lab_ref[1:2,c],1.0,0.0).astype(BF)
        tot=tot+nt(three[:,c],hot)
    out_ref[...]=tot[:16]+tot[16:32]+tot[32:]

def spill(lab,g,rows):
    return pl.pallas_call(
        spill_kernel,
        out_shape=jax.ShapeDtypeStruct((HEADS,rows),F32),
        compiler_params=pltpu.CompilerParams(vmem_limit_bytes=VM),
        name="table_rows", cost_estimate=cost(5),
    )(lab,g)


BLOCK = 32
B_FC1, B_PROJ, GAIN2, BIAS2, B_FC2, GAIN1, BIAS1, B_QV = range(8)
VEC_LANES = {B_FC1: (0, 128), GAIN1: (128, 32), BIAS1: (160, 32), B_QV: (192, 64), B_PROJ: (256, 32), GAIN2: (288, 32), BIAS2: (320, 32), B_FC2: (352, 32)}
VECTOR = 384


def load_weight(own_ref, other_ref, places_ref, held, sem, vecs=None, start=True):
    core = places_ref[64]
    lanes = slice(0, held.shape[2])
    copies = []
    for i in range(16):
        rows = pl.ds(i * BLOCK, BLOCK)
        own = own_ref.at[places_ref[i]]
        copies.append(pltpu.make_async_copy(own.at[:, lanes], held.at[core, rows, :], sem.at[2 * i]))
        copies.append(
            pltpu.make_async_copy(other_ref.at[places_ref[16 + i]].at[:, lanes], held.at[1 - core, rows, :], sem.at[2 * i + 1])
        )
        if vecs is not None:
            copies.append(pltpu.make_async_copy(own.at[0:16, held.shape[2] :], vecs.at[i], sem.at[32 + i]))
    if start:
        for copy in copies:
            copy.start()
    return copies


def await_all(copies):
    for copy in copies:
        copy.wait()


def store_grad(total, places_ref, own_ref, send_ref):
    core = places_ref[64]

    def block(i, carry):
        own_ref[i, :, : total.shape[2]] = total[core, pl.ds(pl.multiple_of(places_ref[32 + i] * BLOCK, BLOCK), BLOCK), :].astype(BF)
        send_ref[i, :, : total.shape[2]] = total[1 - core, pl.ds(pl.multiple_of(places_ref[48 + i] * BLOCK, BLOCK), BLOCK), :].astype(BF)
        return carry

    lax.fori_loop(0, 16, block, 0)


def normalise(values):
    mean = jnp.mean(values, axis=-1, keepdims=True)
    centred = values - mean
    inverse = lax.rsqrt(jnp.mean(centred * centred, axis=-1, keepdims=True) + EPS)
    return centred * inverse, inverse


def project_kernel(
    places_ref, x_ref, own_ref, other_ref, q_ref, kt_ref, vt_ref, k_ref, v_ref, vec_ref, held, loose, sem
):
    @pl.when(pl.program_id(0) == 0)
    def _():
        await_all(load_weight(own_ref, other_ref, places_ref, held, sem, loose))
        rows = [loose[i].astype(F32) for i in range(16)]
        for name, (at, count) in VEC_LANES.items():
            parts = [row[at // 128 : at // 128 + 1, at % 128 : at % 128 + count] for row in rows]
            vec_ref[name : name + 1, : 16 * count] = jnp.concatenate(parts, axis=1)

    width = x_ref.shape[2]
    normed, _ = normalise(x_ref[0].astype(F32))
    first = (normed * vec_ref[GAIN1 : GAIN1 + 1, :width] + vec_ref[BIAS1 : BIAS1 + 1, :width]).astype(BF)
    left, right = nn(first, held[0]), nn(first, held[1])
    half = width // 2
    q = (left[:, :width] + vec_ref[B_QV : B_QV + 1, :width]) * SCALE
    k = jnp.concatenate([left[:, width:], right[:, :half]], axis=1)
    v = right[:, half:] + vec_ref[B_QV : B_QV + 1, width : 2 * width]
    q_ref[0] = jnp.transpose(q.astype(BF))
    kt_ref[0] = jnp.transpose(k.astype(BF))
    vt_ref[0] = jnp.transpose(v.astype(BF))
    k_ref[0] = k.astype(BF)
    v_ref[0] = v.astype(BF)


def project(places, x, own, other, hidden_width):
    nw, n, width = x.shape
    tok = pl.BlockSpec((1, n, width), lambda w, s: (w, 0, 0))
    feat = pl.BlockSpec((1, width, n), lambda w, s: (w, 0, 0))
    anywhere = pl.BlockSpec(memory_space=pl.ANY)
    vecs = (8, hidden_width)
    return pl.pallas_call(
        project_kernel,
        grid_spec=pltpu.PrefetchScalarGridSpec(
            num_scalar_prefetch=1,
            grid=(nw,),
            in_specs=[tok, anywhere, anywhere],
            out_specs=[feat, feat, feat, tok, tok, pl.BlockSpec(vecs, lambda w, s: (0, 0))],
            scratch_shapes=[
                pltpu.VMEM((2, 16 * BLOCK, own.shape[2] - 128), BF),
                pltpu.VMEM((16, 16, 128), BF),
                pltpu.SemaphoreType.DMA((48,)),
            ],
        ),
        out_shape=[jax.ShapeDtypeStruct((nw, width, n), BF)] * 3
        + [jax.ShapeDtypeStruct((nw, n, width), BF)] * 2
        + [jax.ShapeDtypeStruct(vecs, F32)],
        compiler_params=pltpu.CompilerParams(vmem_limit_bytes=VM),
        name="project", cost_estimate=cost(9),
    )(places, x, own, other)


TAIL = (0.254829592, -0.284496736, 1.421413741, -1.453152027, 1.061405429)


def normal_parts(values):
    t = pl.reciprocal(1.0 + (0.3275911 * 0.7071067811865476) * jnp.abs(values), approx=False)
    series = TAIL[4]
    for factor in TAIL[3::-1]:
        series = series * t + factor
    bell = jnp.exp2(values * values * (-0.5 * LOG2E))
    upper = (0.5 * t) * series * bell
    return jnp.where(values >= 0, 1.0 - upper, upper), bell * 0.3989422804014327


def column_sums(values):
    return jnp.sum(values, axis=0, keepdims=True)


def feed_kernel(
    places_ref, x_ref, ctx0_ref, ctx1_ref, og_ref, vec_ref, own_ref, other_ref, out_ref, mid_grad_ref, gt_ref, own_grad_ref,
    send_grad_ref, sums_ref, held, total, wide, thin, projt, sem,
):
    step = pl.program_id(0)

    @pl.when(step == 0)
    def _():
        total[...] = jnp.zeros_like(total)
        sums_ref[...] = jnp.zeros_like(sums_ref)
        await_all(load_weight(own_ref, other_ref, places_ref, held, sem))

    width = x_ref.shape[2]
    half = width // 2

    @pl.when(step == 0)
    def _():
        for j in range(2):
            projt[j] = jnp.transpose(held[j, :, :half].astype(F32)).astype(BF)

    chunk = (held.shape[2] - half) // 2
    vec = lambda row: vec_ref[row : row + 1, :width]
    ctx = (ctx0_ref[0], ctx1_ref[0])
    branch = nt(ctx[0], held[0, :, :half]) + nt(ctx[1], held[1, :, :half])
    mid = x_ref[0].astype(F32) + (branch + vec(B_PROJ))
    normed, inverse = normalise(mid)
    second = normed * vec(GAIN2) + vec(BIAS2)
    second = second.astype(BF)
    second_t = jnp.transpose(second)
    og = og_ref[0]
    og_t = jnp.transpose(og)
    mlp = jnp.zeros(mid.shape, F32)
    second_grad = jnp.zeros(mid.shape, F32)
    piece = chunk // 2
    cuts = []
    for j in range(2):
        for part in range(2):
            at = half + part * piece
            cuts.append((j, slice(at, at + piece), slice(at + chunk, at + chunk + piece), slice(j * chunk + part * piece, j * chunk + (part + 1) * piece)))

    def widen(i):
        j, c1, c2, cols = cuts[i]
        wide[0, i % 2] = nn(second, held[j, :, c1]) + vec_ref[B_FC1 : B_FC1 + 1, cols]
        wide[1, i % 2] = nn(og, held[j, :, c2])

    widen(0)
    for i, (j, c1, c2, cols) in enumerate(cuts):
        hidden = wide[0, i % 2]
        phi_sum, density = normal_parts(hidden)
        thin[0, i % 2] = (hidden * phi_sum).astype(BF)
        hidden_grad = wide[1, i % 2] * (phi_sum + hidden * density)
        sums_ref[0:1, cols] += column_sums(hidden_grad)
        thin[1, i % 2] = hidden_grad.astype(BF)
        if i + 1 < len(cuts):
            widen(i + 1)
        mlp += nt(thin[0, i % 2], held[j, :, c2])
        second_grad += nt(thin[1, i % 2], held[j, :, c1])
        total[j, :, c1] += nn(second_t, thin[1, i % 2])
        total[j, :, c2] += nn(og_t, thin[0, i % 2])
    out_ref[0] = (mid + (mlp + vec(B_FC2))).astype(BF)
    scaled = second_grad * vec(GAIN2)
    inner = jnp.mean(scaled, axis=-1, keepdims=True)
    along = jnp.mean(scaled * normed, axis=-1, keepdims=True)
    og = og.astype(F32)
    mid_grad = og + inverse * (scaled - inner - normed * along)
    mid_grad_ref[0] = mid_grad
    low = mid_grad.astype(BF)
    sums_ref[1:2, :width] += column_sums(mid_grad)
    sums_ref[2:3, :width] += column_sums(second_grad * normed)
    sums_ref[3:4, :width] += column_sums(second_grad)
    sums_ref[4:5, :width] += column_sums(og)
    low_t = jnp.transpose(low)
    for j in range(2):
        total[j, :, :half] += nn(low_t, ctx[j])
        proj = projt[j]
        gt_ref[0, j * half : (j + 1) * half, :] = nn(proj, low_t).astype(BF)

    @pl.when(step == pl.num_programs(0) - 1)
    def _():
        store_grad(total, places_ref, own_grad_ref, send_grad_ref)


def feed(places, x, ctx0, ctx1, og, vecs, own, other):
    nw, n, width = x.shape
    tok = pl.BlockSpec((1, n, width), lambda w, s: (w, 0, 0))
    feat = pl.BlockSpec((1, width, n), lambda w, s: (w, 0, 0))
    whole = pl.BlockSpec(own.shape, lambda w, s: (0, 0, 0))
    anywhere = pl.BlockSpec(memory_space=pl.ANY)
    side = pl.BlockSpec((1, n, width // 2), lambda w, s: (w, 0, 0))
    hidden_width = own.shape[2] - width // 2
    return pl.pallas_call(
        feed_kernel,
        grid_spec=pltpu.PrefetchScalarGridSpec(
            num_scalar_prefetch=1,
            grid=(nw,),
            in_specs=[tok, side, side, tok, pl.BlockSpec(vecs.shape, lambda w, s: (0, 0)), anywhere, anywhere],
            out_specs=[tok, tok, feat, whole, whole, pl.BlockSpec((8, hidden_width), lambda w, s: (0, 0))],
            scratch_shapes=[
                pltpu.VMEM((2, 16 * BLOCK, own.shape[2]), BF),
                pltpu.VMEM((2, 16 * BLOCK, own.shape[2]), F32),
                pltpu.VMEM((2, 2, n, hidden_width // 4), F32),
                pltpu.VMEM((2, 2, n, hidden_width // 4), BF),
                pltpu.VMEM((2, width // 2, 16 * BLOCK), BF),
                pltpu.SemaphoreType.DMA((32,)),
            ],
        ),
        out_shape=[
            jax.ShapeDtypeStruct((nw, n, width), BF),
            jax.ShapeDtypeStruct((nw, n, width), F32),
            jax.ShapeDtypeStruct((nw, width, n), BF),
            jax.ShapeDtypeStruct(own.shape, BF),
            jax.ShapeDtypeStruct(own.shape, BF),
            jax.ShapeDtypeStruct((8, hidden_width), F32),
        ],
        compiler_params=pltpu.CompilerParams(vmem_limit_bytes=VM),
        name="feed_forward", cost_estimate=cost(44),
    )(places, x, ctx0, ctx1, og, vecs, own, other)


def input_kernel(
    places_ref, x_ref, dq0, dk0, dv0, dq1, dk1, dv1, mid_grad_ref, vec_ref, fc_sums_ref,
    own_ref, other_ref, out_ref, own_grad_ref, send_grad_ref, held, total, sums, small, sem,
):
    step = pl.program_id(0)

    @pl.when(step == 0)
    def _():
        total[...] = jnp.zeros_like(total)
        sums[...] = jnp.zeros_like(sums)
        load_weight(own_ref, other_ref, places_ref, held, sem)

    width = x_ref.shape[2]
    half = width // 2
    vec = lambda row: vec_ref[row : row + 1, :width]
    normed, inverse = normalise(x_ref[0].astype(F32))
    first_t = jnp.transpose((normed * vec(GAIN1) + vec(BIAS1)).astype(BF))
    left = jnp.concatenate([dq0[0], dq1[0], dk0[0]], axis=1)
    right = jnp.concatenate([dk1[0], dv0[0], dv1[0]], axis=1)
    total[0] += nn(first_t, left)
    total[1] += nn(first_t, right)

    @pl.when(step == 0)
    def _():
        await_all(load_weight(own_ref, other_ref, places_ref, held, sem, start=False))

    first_grad = (nt(left, held[0]) + nt(right, held[1])).astype(BF).astype(F32)
    scaled = first_grad * vec(GAIN1)
    inner = jnp.mean(scaled, axis=-1, keepdims=True)
    along = jnp.mean(scaled * normed, axis=-1, keepdims=True)
    out_ref[0] = (mid_grad_ref[0] + inverse * (scaled - inner - normed * along)).astype(BF)
    sums[0:1, :width] += column_sums(first_grad * normed)
    sums[1:2, :width] += column_sums(first_grad)
    sums[2:3, :width] += column_sums(left[:, :width].astype(F32))
    sums[2:3, width:] += column_sums(right[:, half:].astype(F32))

    @pl.when(step == pl.num_programs(0) - 1)
    def _():
        columns = total.shape[2]
        store_grad(total, places_ref, own_grad_ref, send_grad_ref)
        rows = {
            B_FC1: fc_sums_ref[0:1, :], B_PROJ: fc_sums_ref[1:2, :], GAIN2: fc_sums_ref[2:3, :], BIAS2: fc_sums_ref[3:4, :],
            B_FC2: fc_sums_ref[4:5, :], GAIN1: sums[0:1, :], BIAS1: sums[1:2, :], B_QV: sums[2:3, :],
        }
        for i in range(16):
            parts = [rows[name][:, i * count : (i + 1) * count] for name, (_, count) in VEC_LANES.items()]
            line = jnp.concatenate(parts, axis=1)
            small[i] = jnp.concatenate([line[:, :128], line[:, 128:256], line[:, 256:], jnp.zeros((BLOCK - 3, 128), F32)], axis=0)

        def block(i, carry):
            own_grad_ref[i, :, columns:] = small[places_ref[32 + i]].astype(BF)
            send_grad_ref[i, :, columns:] = small[places_ref[48 + i]].astype(BF)
            return carry

        lax.fori_loop(0, 16, block, 0)


def input_side(places, x, groups, mid_grad, vecs, fc_sums, own, other):
    nw, n, width = x.shape
    tok = pl.BlockSpec((1, n, width), lambda w, s: (w, 0, 0))
    part = pl.BlockSpec((1, n, width // 2), lambda w, s: (w, 0, 0))
    flat = lambda shape: pl.BlockSpec(shape, lambda w, s: (0,) * len(shape))
    anywhere = pl.BlockSpec(memory_space=pl.ANY)
    columns = own.shape[2] - 128
    grad = own.shape
    return pl.pallas_call(
        input_kernel,
        grid_spec=pltpu.PrefetchScalarGridSpec(
            num_scalar_prefetch=1,
            grid=(nw,),
            in_specs=[tok] + [part] * 6 + [tok, flat(vecs.shape), flat(fc_sums.shape), anywhere, anywhere],
            out_specs=[tok, flat(grad), flat(grad)],
            scratch_shapes=[
                pltpu.VMEM((2, 16 * BLOCK, columns), BF),
                pltpu.VMEM((2, 16 * BLOCK, columns), F32),
                pltpu.VMEM((8, 2 * width), F32),
                pltpu.VMEM((16, BLOCK, 128), F32),
                pltpu.SemaphoreType.DMA((32,)),
            ],
        ),
        out_shape=[
            jax.ShapeDtypeStruct((nw, n, width), BF),
            jax.ShapeDtypeStruct(grad, BF),
            jax.ShapeDtypeStruct(grad, BF),
        ],
        compiler_params=pltpu.CompilerParams(vmem_limit_bytes=VM),
        name="input_side", cost_estimate=cost(15),
    )(places, x, *[part for group in groups for part in group[:3]], mid_grad, vecs, fc_sums, own, other)


def from_partner(shard, axis, stride):
    return lax.ppermute(shard, axis, [(i, i ^ 1 << stride) for i in range(lax.axis_size(axis))])


def to_block(windows, local_count):
    clip_count, chans = (windows.shape[0], windows.shape[-1])
    parted = windows.reshape(
        clip_count, local_count[0], local_count[1], local_count[2], WT, WH, WW, chans
    )
    parted = parted.transpose(0, 1, 4, 2, 5, 3, 6, 7)
    return parted.reshape(
        clip_count, local_count[0] * WT, local_count[1] * WH, local_count[2] * WW, chans
    )


def from_block(block, local_count):
    clip_count, chans = (block.shape[0], block.shape[-1])
    parted = block.reshape(
        clip_count, local_count[0], WT, local_count[1], WH, local_count[2], WW, chans
    )
    parted = parted.transpose(0, 1, 3, 5, 2, 4, 6, 7)
    return parted.reshape(clip_count, -1, WT * WH * WW, chans)


def roll_ahead(windows, local_count, bit_list):
    block = to_block(windows, local_count)
    for grid_dim, amount, bit_pos in (
        (1, WT // 2, bit_list[0]),
        (2, WH // 2, bit_list[1]),
        (3, WW // 2, bit_list[2]),
    ):
        if bit_pos < 0:
            block = jnp.roll(block, -amount, axis=grid_dim)
        else:
            front = lax.slice_in_dim(block, 0, amount, axis=grid_dim)
            arrived = from_partner(front, "seq", bit_pos)
            rest = lax.slice_in_dim(block, amount, block.shape[grid_dim], axis=grid_dim)
            block = jnp.concatenate([rest, arrived], axis=grid_dim)
    return from_block(block, local_count)


def roll_behind(windows, local_count, bit_list):
    block = to_block(windows, local_count)
    for grid_dim, amount, bit_pos in (
        (1, WT // 2, bit_list[0]),
        (2, WH // 2, bit_list[1]),
        (3, WW // 2, bit_list[2]),
    ):
        if bit_pos < 0:
            block = jnp.roll(block, amount, axis=grid_dim)
        else:
            extent = block.shape[grid_dim]
            trailing = lax.slice_in_dim(block, extent - amount, extent, axis=grid_dim)
            arrived = from_partner(trailing, "seq", bit_pos)
            rest = lax.slice_in_dim(block, 0, extent - amount, axis=grid_dim)
            block = jnp.concatenate([arrived, rest], axis=grid_dim)
    return from_block(block, local_count)


KEEP = WT // 2 * WH * WW


def hwt_order():
    place = np.arange(WIN_TOK)
    return (place % WT * WH + place // (WW * WT)) * WW + place // WT % WW


def order_ones(shift):
    place = np.arange(WIN_TOK)
    out = np.zeros((WIN_TOK, WIN_TOK), np.float32)
    out[place, ((place + shift) % WT * WH + place // (WW * WT)) * WW + place // WT % WW] = 1
    return out


def tile_runs(win):
    runs = []
    for c in range(WH):
        h = (win // 2 * WH + c + WH // 2) % (2 * WH)
        for e, count in ((0, WW - WW // 2), (WW - WW // 2, WW // 2)):
            w = (win % 2 * WW + e + WW // 2) % (2 * WW)
            runs.append((h // WH * 2 + w // WW, h % WH * WW + w % WW, count))
    return runs


def swap_cores(part):
    return lax.ppermute(part, "seq", [(0, 1), (1, 0)])


def enter_kernel(own_ref, arrived_ref, order_ref, out_ref, held):
    _, n, width = own_ref.shape
    rows = lax.broadcasted_iota(jnp.int32, (n, width), 0)
    for source in range(4):
        values = jnp.where(rows >= KEEP, own_ref[source].astype(F32), arrived_ref[source].astype(F32)).astype(BF)
        held[source] = nn(order_ref[...], values)
    for win in range(4):
        parts = [held[source, 8 * at : 8 * (at + count), :] for source, at, count in tile_runs(win)]
        out_ref[win] = jnp.concatenate(parts, axis=0).astype(BF)


def leave_kernel(rows_ref, order_ref, out_ref, send_ref, held):
    for win in range(4):
        values = rows_ref[win].astype(F32)
        start = 0
        for source, at, count in tile_runs(win):
            held[source, 8 * at : 8 * (at + count), :] = values[8 * start : 8 * (start + count), :]
            start += count
    for source in range(4):
        values = nn(order_ref[...], held[source].astype(BF)).astype(out_ref.dtype)
        out_ref[source] = values
        send_ref[source] = values[: send_ref.shape[1]].astype(BF)


SENT = 208


def enter(windows, plan, arrived=None):
    clips, wins, toks, width = windows.shape
    if plan["levels"] == 1 and clips == 1:
        own = windows.reshape(wins, toks, width)
        block = (wins, toks, width // 2)
        part = pl.BlockSpec(block, lambda i: (0, 0, i))
        return pl.pallas_call(
            enter_kernel,
            grid=(2,),
            in_specs=[part, part, pl.BlockSpec((toks, toks), lambda i: (0, 0))],
            out_specs=part,
            out_shape=jax.ShapeDtypeStruct(own.shape, BF),
            scratch_shapes=[pltpu.VMEM(block, F32)],
            compiler_params=pltpu.CompilerParams(vmem_limit_bytes=VM),
            name="enter", cost_estimate=cost(4),
        )(own, arrived.reshape(own.shape), plan["order"])
    rolled = roll_ahead(windows, plan["local"], plan["bits"])
    rolled = rolled.reshape(clips * wins, WT, WH * WW, width).transpose(0, 2, 1, 3)
    return rolled.reshape(clips * wins, toks, width)


def leave(windows, plan, kind):
    wins, toks, width = windows.shape
    block = (wins, toks, width // 2)
    part = pl.BlockSpec(block, lambda i: (0, 0, i))
    return pl.pallas_call(
        leave_kernel,
        grid=(2,),
        in_specs=[part, pl.BlockSpec((toks, toks), lambda i: (0, 0))],
        out_specs=[part, pl.BlockSpec((wins, SENT, width // 2), lambda i: (0, 0, i))],
        out_shape=[jax.ShapeDtypeStruct(windows.shape, kind), jax.ShapeDtypeStruct((wins, SENT, width), BF)],
        scratch_shapes=[pltpu.VMEM(block, F32)],
        compiler_params=pltpu.CompilerParams(vmem_limit_bytes=VM),
        name="leave", cost_estimate=cost(4),
    )(windows, plan["order"].T)


def joined(kept, arrived):
    arrived = jnp.pad(arrived.astype(kept.dtype), ((0, 0), (0, kept.shape[1] - SENT), (0, 0)))
    rows = lax.broadcasted_iota(jnp.int32, kept.shape, 1)
    return jnp.where(rows < KEEP, arrived, kept)[None]


def leave_any(windows, plan, clips, kind):
    count, toks, width = windows.shape
    wins = count // clips
    if plan["levels"] == 1 and clips == 1:
        kept, sent = leave(windows, plan, kind)
        return joined(kept, swap_cores(sent))
    rows = windows.reshape(count, WH * WW, WT, width).transpose(0, 2, 1, 3)
    return roll_behind(rows.reshape(clips, wins, toks, width), plan["local"], plan["bits"]).astype(kind)


def pack_kernel(core_ref, qkv_ref, proj_ref, fc1_ref, fc2_ref, *rest):
    vec_refs, (qkv_out, fc_out) = rest[:-2], rest[-2:]

    def emit(side):
        half = qkv_ref.shape[1] // 2
        qkv_out[:, :half] = qkv_ref[:, side * half : (side + 1) * half]
        at = 0
        for ref in (proj_ref, fc1_ref, fc2_ref):
            half = ref.shape[1] // 2
            fc_out[:, at : at + half] = ref[:, side * half : (side + 1) * half]
            at += half

    half = qkv_ref.shape[1] // 2
    line = jnp.concatenate([ref[...].astype(F32).reshape(1, -1) for ref in vec_refs], axis=1)
    lines = [line[:, at : at + 128] for at in range(0, VECTOR, 128)]
    qkv_out[:, half:] = jnp.concatenate(lines + [jnp.zeros((BLOCK - len(lines), 128), F32)], axis=0).astype(BF)
    for side in range(2):
        @pl.when(core_ref[0] == side)
        def _():
            emit(side)


def pack(core, qkv, proj_t, fc1, fc2_t, vectors):
    columns = (proj_t.shape[1] + fc1.shape[1] + fc2_t.shape[1]) // 2
    vmem = pl.BlockSpec(memory_space=pltpu.VMEM)
    return pl.pallas_call(
        pack_kernel,
        in_specs=[pl.BlockSpec(memory_space=pltpu.SMEM)] + [vmem] * (4 + len(vectors)),
        out_shape=[
            jax.ShapeDtypeStruct((BLOCK, qkv.shape[1] // 2 + 128), BF),
            jax.ShapeDtypeStruct((BLOCK, columns), BF),
        ],
        compiler_params=pltpu.CompilerParams(vmem_limit_bytes=VM),
        name="pack", cost_estimate=cost(2),
    )(core, qkv, proj_t, fc1, fc2_t, *vectors)


def hop(part, flips):
    pairs = [(16 * c + s, 16 * c + (s ^ flips[c])) for c in range(2) for s in range(16)]
    return lax.ppermute(part, ("seq", "shard"), pairs)


def tree_places():
    me = lax.axis_index("shard")
    core = lax.axis_index("seq")
    entry = jnp.arange(16, dtype=jnp.int32)
    v, u, z = entry // 8, entry // 4 % 2, entry % 4
    straight, crossed = me ^ (4 * z + 2 * u + v), me ^ (4 * z + 2 * v + u)
    rel = me ^ entry
    z, y, x = rel // 4, rel // 2 % 2, rel % 2
    place_straight, place_crossed = x * 8 + y * 4 + z, y * 8 + x * 4 + z
    even = core == 0
    pick_core = lambda left, right: jnp.where(even, left, right)
    return jnp.concatenate(
        [
            pick_core(place_straight, place_crossed),
            pick_core(place_crossed, place_straight),
            pick_core(straight, crossed),
            pick_core(crossed, straight),
            jnp.broadcast_to(core, (1,)),
        ]
    ).astype(jnp.int32)


def tree_gather(part):
    arrived = yield [hop(part, (4 * k, 4 * k)) for k in range(1, 4)]
    stack = jnp.stack([part] + arrived)
    arrived = yield hop(stack, (2, 1))
    stack = jnp.concatenate([stack, arrived])
    arrived = yield hop(stack, (1, 2))
    stack = jnp.concatenate([stack, arrived])
    other = yield swap_cores(stack)
    yield stack, other


def tie(*items):
    return lax.optimization_barrier(items)


def add_low(left, right):
    return (left.astype(F32) + right.astype(F32)).astype(BF)


def tree_scatter(own, send):
    arrived = yield swap_cores(send)
    stack = add_low(own, arrived)
    arrived = yield hop(stack[8:], (1, 2))
    stack = add_low(stack[:8], arrived)
    arrived = yield hop(stack[4:], (2, 1))
    stack = add_low(stack[:4], arrived)
    arrived = yield [hop(stack[k], (4 * k, 4 * k)) for k in range(1, 4)]
    arrived = [part.astype(F32) for part in arrived]
    yield (stack[0].astype(F32) + arrived[0]) + (arrived[1] + arrived[2])


def finish(steps, pending):
    while True:
        try:
            pending = steps.send(pending)
        except StopIteration:
            return pending


def table_sum(table):
    for axis, flip in (("seq", 1), ("shard", 1), ("shard", 2)):
        pairs = [(i, i ^ flip) for i in range(2 if axis == "seq" else 16)]
        arrived = yield lax.ppermute(table, axis, pairs)
        table = add_low(table, arrived)
    arrived = yield [hop(table, (4 * k, 4 * k)) for k in range(1, 4)]
    arrived = [part.astype(F32) for part in arrived]
    yield (table.astype(F32) + arrived[0]) + (arrived[1] + arrived[2])


def sides(part, other, core):
    other = other.astype(F32)
    return [jnp.where(core == 0, part, other), jnp.where(core == 0, other, part)]


def body(
    tokens, norm1_gain, norm1_bias, qkv_weight, qv_bias, position_table, proj_weight, proj_bias, norm2_gain,
    norm2_bias, fc1_weight, fc1_bias, fc2_weight, fc2_bias, rel_index, region_ids, cotangent,
):
    levels = lax.axis_size("seq").bit_length() - 1
    clips, wins, toks, width = tokens.shape
    hidden_width = fc1_weight.shape[1]
    plan = {
        "levels": levels,
        "local": [1 if levels > level_pos else 2 for level_pos in range(3)],
        "bits": [levels - 1 - level_pos for level_pos in range(3)],
        "order": jnp.asarray(order_ones(WT // 2), BF),
    }

    def fc_outputs(pair):
        cut = (width // 2, (width + hidden_width) // 2)
        return [jnp.concatenate(two, axis=1) for two in zip(*(jnp.split(part, cut, axis=1) for part in pair))]

    vectors = [fc1_bias, norm1_gain, norm1_bias, qv_bias, proj_bias, norm2_gain, norm2_bias, fc2_bias]
    sizes = [part.shape[0] for part in vectors]
    spread = jnp.asarray(spread_ones(), BF)
    spots = jnp.asarray(spread_spots())
    wide8 = jnp.asarray(lane16(False).T, BF)
    wide16 = jnp.asarray(lane16(True), BF)
    maps = jnp.asarray(np.stack(lane_maps(False) + lane_maps(True)))
    table = prepare(rel_index, maps, position_table.T, region_ids, jnp.asarray(order_ones(0), BF), wide8)
    if clips == 1 and lax.axis_size("shard") == 16 and lax.axis_size("seq") == 2:
        core = lax.axis_index("seq")
        places = tree_places()
        qkv_part, fc_part = pack(
            jnp.reshape(core, (1,)), qkv_weight, proj_weight.T, fc1_weight, fc2_weight.T, vectors
        )
        qkv_steps, fc_steps = tree_gather(qkv_part), tree_gather(fc_part)
        qkv_hop = next(qkv_steps)
        arrived = swap_cores(tokens)
        table, qkv_hop, arrived = tie(table, qkv_hop, arrived)
        labels, narrow, mask_keys, mask_queries = table
        qkv_hop = qkv_steps.send(qkv_hop)
        shifted = enter(tokens, plan, arrived)
        qkv_hop, shifted, narrow, fc_part = tie(qkv_hop, shifted, narrow, fc_part)
        qkv_hop = qkv_steps.send(qkv_hop)
        fc_hop = next(fc_steps)
        bias_low = bias_half(0, narrow, spots)
        arrived = swap_cores(cotangent)
        qkv_hop, bias_low, arrived, narrow = tie(qkv_hop, bias_low, arrived, narrow)
        qkv_hop = qkv_steps.send(qkv_hop)
        out_grad = enter(cotangent, plan, arrived)
        qkv_hop, out_grad, fc_hop = tie(qkv_hop, out_grad, fc_hop)
        qkv_own, qkv_other = qkv_steps.send(qkv_hop)
        fc_hop = fc_steps.send(fc_hop)
        q_t, k_t, v_t, token_k, token_v, vecs = project(places, shifted, qkv_own, qkv_other, hidden_width)
        q_t, fc_hop = tie(q_t, fc_hop)
        fc_hop = fc_steps.send(fc_hop)
        low = attend(0, q_t, token_k, v_t, bias_low, mask_queries, mask_keys)
        narrow, low = tie(narrow, low)
        bias_high = bias_half(1, narrow, spots)
        q_t, low, fc_hop, bias_high = tie(q_t, low, fc_hop, bias_high)
        fc_hop = fc_steps.send(fc_hop)
        high = attend(1, q_t, token_k, v_t, bias_high, mask_queries, mask_keys)
        high, fc_hop = tie(high, fc_hop)
        fc_own, fc_other = fc_steps.send(fc_hop)
        block_out, mid_grad, context_grad_t, fc_keep, fc_send, fc_sums = feed(
            places, shifted, low[1], high[1], out_grad, vecs, fc_own, fc_other
        )
        fc_steps = tree_scatter(fc_keep, fc_send)
        fc_hop = next(fc_steps)
        groups = []
        for side, (context_t, _, expo, inverse_sum) in enumerate((low, high)):
            group = attend_back(
                side, expo, k_t, token_v, q_t, context_grad_t, context_t, inverse_sum, spread, wide16
            )
            group, fc_hop, context_grad_t, block_out = tie(group, fc_hop, context_grad_t, block_out)
            groups.append(group)
            fc_hop = fc_steps.send(fc_hop)
        offsets = jnp.concatenate([group[3] for group in groups]).reshape(HEADS, WIDE)
        table_steps = table_sum(offsets.astype(BF))
        table_hop = next(table_steps)
        input_grad, qkv_keep, qkv_send = input_side(
            places, shifted, groups, mid_grad, vecs, fc_sums, qkv_own, qkv_other
        )
        input_grad, qkv_send, fc_hop, table_hop, block_out = tie(input_grad, qkv_send, fc_hop, table_hop, block_out)
        qkv_steps = tree_scatter(qkv_keep, qkv_send)
        qkv_hop = next(qkv_steps)
        fc_hop = fc_steps.send(fc_hop)
        table_hop = table_steps.send(table_hop)
        kept, sent = leave(input_grad, plan, F32)
        qkv_hop, table_hop, kept, sent, block_out = tie(qkv_hop, table_hop, kept, sent, block_out)
        qkv_hop = qkv_steps.send(qkv_hop)
        table_hop = table_steps.send(table_hop)
        arrived = swap_cores(sent)
        out_kept, out_sent = leave(block_out, plan, BF)
        qkv_hop, table_hop, fc_hop, arrived, out_kept, out_sent = tie(qkv_hop, table_hop, fc_hop, arrived, out_kept, out_sent)
        qkv_hop = qkv_steps.send(qkv_hop)
        table_hop = table_steps.send(table_hop)
        own_fc = finish(fc_steps, fc_hop)
        out_arrived = swap_cores(out_sent)
        fc_swap = swap_cores(own_fc.astype(BF))
        input_grad = joined(kept, arrived)
        qkv_hop, table_hop, input_grad, fc_swap, out_arrived = tie(qkv_hop, table_hop, input_grad, fc_swap, out_arrived)
        qkv_hop = qkv_steps.send(qkv_hop)
        offsets = finish(table_steps, table_hop)
        block_out = joined(out_kept, out_arrived)
        own_fc = fc_outputs(sides(own_fc, fc_swap, core))
        table_grad = spill(labels, offsets, position_table.shape[0])
        qkv_hop, block_out, own_fc, table_grad = tie(qkv_hop, block_out, own_fc, table_grad)
        own_qkv = finish(qkv_steps, qkv_hop)
        small = own_qkv[: VECTOR // 128, width * 3 // 2 :].reshape(-1)
        own_qkv = own_qkv[:, : width * 3 // 2]
        own_qkv = sides(own_qkv, swap_cores(own_qkv.astype(BF)), core)
    else:
        straight = np.arange(16)
        places = jnp.asarray(np.concatenate([straight, straight, straight, straight, np.zeros(1)]), jnp.int32)
        gather = lambda part: lax.all_gather(part, "shard", axis=0, tiled=True)
        halves = lambda part: jnp.split(part, 2, axis=1)
        parts = [halves(gather(part)) for part in (proj_weight.T, fc1_weight, fc2_weight.T)]
        fc_own, fc_other = (jnp.concatenate(pair, axis=1).reshape(16, BLOCK, -1) for pair in zip(*parts))
        rows = lax.all_gather(jnp.concatenate(vectors), "shard", axis=0, tiled=False)
        pieces = [piece.reshape(16, -1) for piece in jnp.split(rows, np.cumsum(sizes)[:-1], axis=1)]
        rows = jnp.pad(jnp.concatenate(pieces, axis=1).reshape(16, -1, 128), ((0, 0), (0, BLOCK - VECTOR // 128), (0, 0)))
        qkv_own, qkv_other = (
            jnp.concatenate([part.reshape(16, BLOCK, -1), rows], axis=2) for part in halves(gather(qkv_weight))
        )
        shifted = enter(tokens, plan, swap_cores(tokens) if levels == 1 else None)
        out_grad = enter(cotangent, plan, swap_cores(cotangent) if levels == 1 else None)
        labels, narrow, mask_keys, mask_queries = table
        bias_low, bias_high = (bias_half(side, narrow, spots) for side in range(2))
        q_t, k_t, v_t, token_k, token_v, vecs = project(places, shifted, qkv_own, qkv_other, hidden_width)
        low = attend(0, q_t, token_k, v_t, bias_low, mask_queries, mask_keys)
        high = attend(1, q_t, token_k, v_t, bias_high, mask_queries, mask_keys)
        block_out, mid_grad, context_grad_t, fc_keep, fc_send, fc_sums = feed(
            places, shifted, low[1], high[1], out_grad, vecs, fc_own, fc_other
        )
        groups = [
            attend_back(side, expo, k_t, token_v, q_t, context_grad_t, context_t, inverse_sum, spread, wide16)
            for side, (context_t, _, expo, inverse_sum) in enumerate((low, high))
        ]
        input_grad, qkv_keep, qkv_send = input_side(
            places, shifted, groups, mid_grad, vecs, fc_sums, qkv_own, qkv_other
        )
        block_out = leave_any(block_out, plan, clips, BF)
        input_grad = leave_any(input_grad, plan, clips, F32)
        offsets = jnp.concatenate([group[3] for group in groups]).reshape(HEADS, WIDE)
        table_grad = spill(labels, lax.psum(offsets, ("seq", "shard")), position_table.shape[0])
        small = qkv_keep[:, : VECTOR // 128, width * 3 // 2 :].reshape(16, VECTOR)
        small = lax.psum(small.astype(F32), ("seq", "shard"))
        pieces = jnp.split(small, np.cumsum([count for _, count in VEC_LANES.values()])[:-1], axis=1)
        shards = lax.axis_size("shard")
        small = jnp.concatenate([piece.reshape(shards, -1) for piece in pieces], axis=1)
        small = lax.dynamic_index_in_dim(small, lax.axis_index("shard"), 0, keepdims=False)

        def owned(grad):
            grad = lax.psum(grad.reshape(16 * BLOCK, -1), "seq")
            return lax.psum_scatter(grad, "shard", scatter_dimension=0, tiled=True).astype(F32)

        own_fc = fc_outputs([owned(fc_keep), owned(fc_send)])
        own_qkv = [owned(qkv_keep[:, :, : width * 3 // 2]), owned(qkv_send[:, :, : width * 3 // 2])]
    own_proj, own_fc1, own_fc2 = own_fc
    own_qkv = jnp.concatenate(own_qkv, axis=1)
    own_f1b, own_g1, own_b1, own_qv, own_pb, own_g2, own_b2, own_f2b = jnp.split(small, np.cumsum(sizes)[:-1])
    return (
        block_out, input_grad, own_g1, own_b1, own_qkv, own_qv, table_grad.T, own_proj.T, own_pb,
        own_g2, own_b2, own_fc1, own_f1b, own_fc2.T, own_f2b,
    )


def solution(mesh):
    return jax.shard_map(
        body,
        mesh=mesh,
        in_specs=(
            P("shard", "seq", None, None),
            P("shard"),
            P("shard"),
            P("shard", None),
            P("shard"),
            P(),
            P(None, "shard"),
            P("shard"),
            P("shard"),
            P("shard"),
            P("shard", None),
            P("shard"),
            P(None, "shard"),
            P("shard"),
            P(),
            P("seq", None),
            P("shard", "seq", None, None),
        ),
        out_specs=(
            P("shard", "seq", None, None),
            P("shard", "seq", None, None),
            P("shard"),
            P("shard"),
            P("shard", None),
            P("shard"),
            P(),
            P(None, "shard"),
            P("shard"),
            P("shard"),
            P("shard"),
            P("shard", None),
            P("shard"),
            P(None, "shard"),
            P("shard"),
        ),
        check_vma=False,
    )
```

profile of v0, /device:TPU:0, one launch (start us, length us, event | category | flops | bytes accessed | tf_op | source)
XLA Modules:
  0.0 243.8 jit_solution(14843669591474234949)
XLA Ops:
  0.7 0.5 collective-permute-start.3
  1.2 1.9 pack.1
  3.0 2.6 %collective-permute-start = (bf16[32,896]{1,0:T(8,128)(2,1)}, bf16[32,896]{1,0:T(8,128)(2,1)S(1)}, u32[]{:S(2)}, u32[]{:S(2)}) collective-permute-start(bf16[32,896]{1,0:T(8,128)(2,1)} %get-tuple-element.141), channel_id=1, source_target_pairs={{0,4},{1,5},{2,6},{3,7},{4,0},{5,1},{6,2},{7,3},{8,12},{9,13},{10,... | collective-permute-start | bytes 172040 | tf_op jit(solution)/shard_map/ppermute | solution.py:922
  5.6 2.6 %collective-permute-start.1 = (bf16[32,896]{1,0:T(8,128)(2,1)}, bf16[32,896]{1,0:T(8,128)(2,1)S(1)}, u32[]{:S(2)}, u32[]{:S(2)}) collective-permute-start(bf16[32,896]{1,0:T(8,128)(2,1)} %get-tuple-element.141), channel_id=1, source_target_pairs={{0,8},{1,9},{2,10},{3,11},{4,12},{5,13},{6,14},{7,15},{8,0},{9,1},... | collective-permute-start | bytes 172040 | tf_op jit(solution)/shard_map/ppermute | solution.py:922
  8.2 0.9 collective-permute-start.8
  9.1 1.5 constant_dynamic-update-slice_fusion.4
  10.6 6.5 %prepare.1 = (s32[2,2816]{1,0:T(2,128)}, f32[128,1408]{1,0:T(8,128)}, bf16[4,392,128]{2,1,0:T(8,128)(2,1)}, bf16[4,32,392]{2,1,0:T(8,128)(2,1)}) custom-call(s32[392,392]{1,0:T(8,128)} %rel_ref.1, s32[4,2816]{1,0:T(4,128)} %constant.116.clone.maps_ref, bf16[16,2535]{1,0:T(8,128)(2,1)} %bitcast.85, s32[4,392]{1,0:T(4,128)} %region_ref.1, ...), custom_call_target="tpu_custom_call" | custom-call | flops 6000000000 | bytes 21600000 | tf_op jit(solution)/shard_map/prepare/pallas_call | solution.py:312
  17.1 0.6 concatenate.35.places_ref
  17.7 3.5 %collective-permute-start.9 = (bf16[32,2304]{1,0:T(8,128)(2,1)S(1)}, bf16[32,2304]{1,0:T(8,128)(2,1)S(1)}, u32[]{:S(2)}, u32[]{:S(2)}) collective-permute-start(bf16[32,2304]{1,0:T(8,128)(2,1)S(1)} %copy-done.4), channel_id=1, source_target_pairs={{0,8},{1,9},{2,10},{3,11},{4,12},{5,13},{6,14},{7,15},{8,0},{9,1},... | collective-permute-start | bytes 442376 | tf_op jit(solution)/shard_map/ppermute | solution.py:922
  21.4 1.7 collective-permute-start.4
  23.1 0.6 constant_dynamic-update-slice_fusion.3
  23.8 3.8 %enter.2.x_ref = bf16[4,392,512]{2,1,0:T(8,128)(2,1)} custom-call(bf16[4,392,512]{2,1,0:T(8,128)(2,1)} %bitcast.81, bf16[4,392,512]{2,1,0:T(8,128)(2,1)} %bitcast.9.arrived_ref, bf16[392,392]{1,0:T(8,128)(2,1)} %constant.111.clone.order_ref), custom_call_target="tpu_custom_call" | custom-call | flops 4000000000 | bytes 14400000 | tf_op jit(solution)/shard_map/enter/pallas_call | solution.py:836
  27.6 0.6 constant_dynamic-update-slice_fusion.2
  28.2 0.6 constant_dynamic-update-slice_fusion.1
  28.9 0.7 constant_dynamic-update-slice_fusion
  29.6 1.5 collective-permute-start.5
  31.1 5.8 %position_bias.2.bias_ref = bf16[8,392,392]{2,1,0:T(8,128)(2,1)} custom-call(f32[128,1408]{1,0:T(8,128)} %get-tuple-element.178.narrow_ref, s32[392,128]{1,0:T(8,128)} %constant.113.clone.spot_ref), custom_call_target="tpu_custom_call" | custom-call | flops 5000000000 | bytes 18000000 | tf_op jit(solution)/shard_map/position_bias/pallas_call | solution.py:354
  36.9 1.2 collective-permute-done.5
  38.1 0.8 constant_dynamic-update-slice_fusion.5.own_ref
  39.0 3.6 %enter.3.og_ref = bf16[4,392,512]{2,1,0:T(8,128)(2,1)} custom-call(bf16[4,392,512]{2,1,0:T(8,128)(2,1)} %bitcast.82, bf16[4,392,512]{2,1,0:T(8,128)(2,1)} %bitcast.83, bf16[392,392]{1,0:T(8,128)(2,1)} %constant.111.clone.order_ref), custom_call_target="tpu_custom_call" | custom-call | flops 4000000000 | bytes 14400000 | tf_op jit(solution)/shard_map/enter/pallas_call | solution.py:836
  42.6 0.9 copy-done.12
  43.6 0.6 collective-permute-start.11
  44.3 9.5 %project.1 = (bf16[4,512,392]{2,1,0:T(8,128)(2,1)}, bf16[4,512,392]{2,1,0:T(8,128)(2,1)}, bf16[4,512,392]{2,1,0:T(8,128)(2,1)}, bf16[4,392,512]{2,1,0:T(8,128)(2...) custom-call(s32[65]{0:T(128)} %concatenate.35.places_ref, bf16[4,392,512]{2,1,0:T(8,128)(2,1)} %enter.2.x_ref, ...), custom_call_target="tpu_custom_call" | custom-call | flops 8999999488 | bytes 32400000 | tf_op jit(solution)/shard_map/project/pallas_call | solution.py:468
  53.9 1.5 collective-permute-start.12
  55.4 12.5 %attend.2 = (bf16[4,256,392]{2,1,0:T(8,128)(2,1)}, bf16[4,392,256]{2,1,0:T(8,128)(2,1)}, bf16[4,8,392,392]{3,2,1,0:T(8,128)(2,1)}, f32[4,8,392]{2,1,0:T(8,128)}) custom-call(bf16[4,512,392]{2,1,0:T(8,128)(2,1)} %get-tuple-element.182.q_ref, bf16[4,392,512]{2,1,0:T(8,128)(2,1)} %get-tuple-element.164.k_ref, bf16[4,512,392]{2,1,0:T(8,128)(2,1)} %get-tuple-element.165.v_ref, ...), custom_call_target="tpu_custom_call" | custom-call | flops 10000000000 | bytes 36000000 | tf_op jit(solution)/shard_map/attend/pallas_call | solution.py:105
  67.9 5.8 %position_bias.3.bias_ref = bf16[8,392,392]{2,1,0:T(8,128)(2,1)} custom-call(f32[128,1408]{1,0:T(8,128)} %get-tuple-element.178.narrow_ref, s32[392,128]{1,0:T(8,128)} %constant.113.clone.spot_ref), custom_call_target="tpu_custom_call" | custom-call | flops 5000000000 | bytes 18000000 | tf_op jit(solution)/shard_map/position_bias/pallas_call | solution.py:354
  73.8 13.3 %attend.3 = (bf16[4,256,392]{2,1,0:T(8,128)(2,1)}, bf16[4,392,256]{2,1,0:T(8,128)(2,1)}, bf16[4,8,392,392]{3,2,1,0:T(8,128)(2,1)}, f32[4,8,392]{2,1,0:T(8,128)}) custom-call(bf16[4,512,392]{2,1,0:T(8,128)(2,1)} %get-tuple-element.182.q_ref, bf16[4,392,512]{2,1,0:T(8,128)(2,1)} %get-tuple-element.164.k_ref, bf16[4,512,392]{2,1,0:T(8,128)(2,1)} %get-tuple-element.165.v_ref, ...), custom_call_target="tpu_custom_call" | custom-call | flops 10000000000 | bytes 36000000 | tf_op jit(solution)/shard_map/attend/pallas_call | solution.py:105
  87.1 1.4 copy-done.9
  88.5 42.6 %feed_forward.1 = (bf16[4,392,512]{2,1,0:T(8,128)(2,1)}, f32[4,392,512]{2,1,0:T(8,128)}, bf16[4,512,392]{2,1,0:T(8,128)(2,1)}, bf16[16,32,2304]{2,1,0:T(8,128)(2...) custom-call(s32[65]{0:T(128)} %concatenate.35.places_ref, bf16[4,392,512]{2,1,0:T(8,128)(2,1)} %enter.2.x_ref, ...), custom_call_target="tpu_custom_call" | custom-call | flops 44000002048 | bytes 158400000 | tf_op jit(solution)/shard_map/feed_forward/pallas_call | solution.py:596
  131.2 22.5 %attend_back.2 = (bf16[4,392,256]{2,1,0:T(8,128)(2,1)}, bf16[4,392,256]{2,1,0:T(8,128)(2,1)}, bf16[4,392,256]{2,1,0:T(8,128)(2,1)}, f32[2,4,2816]{2,1,0:T(4,128)}) custom-call(bf16[4,8,392,392]{3,2,1,0:T(8,128)(2,1)} %get-tuple-element.179.e_ref, bf16[4,512,392]{2,1,0:T(8,128)(2,1)} %get-tuple-element.180.k_ref, ...), custom_call_target="tpu_custom_call" | custom-call | flops 20000000000 | bytes 72000000 | tf_op jit(solution)/shard_map/attend_back/pallas_call | solution.py:234
  153.8 0.6 add_convert_fusion
  154.5 0.6 collective-permute-start.15
  155.3 22.4 %attend_back.3 = (bf16[4,392,256]{2,1,0:T(8,128)(2,1)}, bf16[4,392,256]{2,1,0:T(8,128)(2,1)}, bf16[4,392,256]{2,1,0:T(8,128)(2,1)}, f32[2,4,2816]{2,1,0:T(4,128)}) custom-call(bf16[4,8,392,392]{3,2,1,0:T(8,128)(2,1)} %get-tuple-element.206.e_ref, bf16[4,512,392]{2,1,0:T(8,128)(2,1)} %get-tuple-element.180.k_ref, ...), custom_call_target="tpu_custom_call" | custom-call | flops 20000000000 | bytes 72000000 | tf_op jit(solution)/shard_map/attend_back/pallas_call | solution.py:234
  178.0 1.6 collective-permute-start.16
  179.8 15.9 %input_side.1 = (bf16[4,392,512]{2,1,0:T(8,128)(2,1)}, bf16[16,32,896]{2,1,0:T(8,128)(2,1)}, bf16[16,32,896]{2,1,0:T(8,128)(2,1)}) custom-call(s32[65]{0:T(128)} %concatenate.35.places_ref, bf16[4,392,512]{2,1,0:T(8,128)(2,1)} %enter.2.x_ref, bf16[4,392,256]{2,1,0:T(8,128)(2,1)} %get-tuple-element.203.dq0, bf16[4,392,256]{2,1,0:T(8,128)(2,1)} %get-tuple-element.204.dk0, ...), custom_call_target="tpu_custom_call" | custom-call | flops 15000000512 | bytes 54000000 | tf_op jit(solution)/shard_map/input_side/pallas_call | solution.py:690
  195.7 0.6 collective-permute-start.18
  196.3 1.4 collective-permute-start.19
  197.8 0.5 collective-permute-start.22
  198.3 3.8 %collective-permute-start.23 = (bf16[32,2304]{1,0:T(8,128)(2,1)S(1)}, bf16[32,2304]{1,0:T(8,128)(2,1)S(1)}, u32[]{:S(2)}, u32[]{:S(2)}) collective-permute-start(bf16[32,2304]{1,0:T(8,128)(2,1)S(1)} %get-tuple-element.270), channel_id=1, source_target_pairs={{0,8},{1,9},{2,10},{3,11},{4,12},{5,13},{6,14},{7,15},{8,0},{9,1},... | collective-permute-start | bytes 442376 | tf_op jit(solution)/shard_map/ppermute | solution.py:922
  202.3 3.8 %leave.2 = (f32[4,392,512]{2,1,0:T(8,128)}, bf16[4,208,512]{2,1,0:T(8,128)(2,1)}) custom-call(bf16[4,392,512]{2,1,0:T(8,128)(2,1)} %get-tuple-element.231.rows_ref, bf16[392,392]{1,0:T(8,128)(2,1)} %constant.124.order_ref), custom_call_target="tpu_custom_call" | custom-call | flops 4000000000 | bytes 14400000 | tf_op jit(solution)/shard_map/leave/pallas_call | solution.py:855
  206.4 0.8 collective-permute-start.20
  207.3 0.6 collective-permute-start.21
  207.9 3.6 %leave.3 = (bf16[4,392,512]{2,1,0:T(8,128)(2,1)}, bf16[4,208,512]{2,1,0:T(8,128)(2,1)}) custom-call(bf16[4,392,512]{2,1,0:T(8,128)(2,1)} %get-tuple-element.239.rows_ref, bf16[392,392]{1,0:T(8,128)(2,1)} %constant.124.order_ref), custom_call_target="tpu_custom_call" | custom-call | flops 4000000000 | bytes 14400000 | tf_op jit(solution)/shard_map/leave/pallas_call | solution.py:855
  211.4 1.7 collective-permute-done.23
  213.1 1.8 collective-permute-done.20
  215.0 0.8 collective-permute-start.27
  215.8 3.4 %collective-permute-start.28 = (bf16[16,2816]{1,0:T(8,128)(2,1)S(1)}, bf16[16,2816]{1,0:T(8,128)(2,1)S(1)}, u32[]{:S(2)}, u32[]{:S(2)}) collective-permute-start(bf16[16,2816]{1,0:T(8,128)(2,1)S(1)} %add_convert_fusion.6), channel_id=1, source_target_pairs={{0,8},{1,9},{2,10},{3,11},{4,12},{5,13},{6,14},{7,15},{8,0},{9,1},... | collective-permute-start | bytes 270344 | tf_op jit(solution)/shard_map/ppermute | solution.py:922
  219.6 0.6 collective-permute-start.26
  220.2 0.6 collective-permute-start.30
  220.8 2.0 select_bitcast_fusion
  222.8 3.5 %collective-permute-done.28 = bf16[16,2816]{1,0:T(8,128)(2,1)S(1)} collective-permute-done((bf16[16,2816]{1,0:T(8,128)(2,1)S(1)}, bf16[16,2816]{1,0:T(8,128)(2,1)S(1)}, u32[]{:S(2)}, u32[]{:S(2)}) %collective-permute-start.28) | collective-permute-done | bytes 90144 | tf_op jit(solution)/shard_map/ppermute | solution.py:922
  226.6 1.7 collective-permute-start.32
  228.4 1.7 collective-permute-start.33
  230.1 1.0 collective-permute-start.34
  231.1 1.6 select_bitcast_fusion.1
  232.6 0.7 pad_maximum_fusion.1
  233.4 0.7 pad_maximum_fusion.2
  234.1 0.7 add_add_fusion.g_ref
  234.8 5.5 %table_rows.1 = f32[16,2535]{1,0:T(8,128)} custom-call(s32[2,2816]{1,0:T(2,128)} %get-tuple-element.254.lab_ref, f32[16,2816]{1,0:T(8,128)} %add_add_fusion.g_ref), custom_call_target="tpu_custom_call" | custom-call | flops 5000000000 | bytes 18000000 | tf_op jit(solution)/shard_map/table_rows/pallas_call | solution.py:380
  240.3 0.6 pad_maximum_fusion.6
  241.0 0.6 fusion.10
  241.6 0.5 slice_bitcast_fusion.9
  242.2 0.6 split.52
  242.9 0.7 pad_maximum_fusion.4
  (111 shorter events, 3.2 us)
Async XLA Ops:
  0.7 20.7 %collective-permute-start.3 = (bf16[1,4,392,512]{3,2,1,0:T(8,128)(2,1)}, bf16[1,4,392,512]{3,2,1,0:T(8,128)(2,1)}, u32[]{:S(2)}, u32[]{:S(2)}) collective-permute-start(bf16[1,4,392,512]{3,2,1,0:T(8,128)(2,1)} %param.24), channel_id=1, source_target_pairs={{0,16},{16,0},{1,17},{17,1},{2,18},{18,2},{3,19},{19,3},{4,20},{20... | collective-permute-start | bytes 4816904 | tf_op jit(solution)/shard_map/ppermute | solution.py:800
  3.0 14.7 %collective-permute-start = (bf16[32,896]{1,0:T(8,128)(2,1)}, bf16[32,896]{1,0:T(8,128)(2,1)S(1)}, u32[]{:S(2)}, u32[]{:S(2)}) collective-permute-start(bf16[32,896]{1,0:T(8,128)(2,1)} %get-tuple-element.141), channel_id=1, source_target_pairs={{0,4},{1,5},{2,6},{3,7},{4,0},{5,1},{6,2},{7,3},{8,12},{9,13},{10,... | collective-permute-start | bytes 172040 | tf_op jit(solution)/shard_map/ppermute | solution.py:922
  5.6 15.6 %collective-permute-start.1 = (bf16[32,896]{1,0:T(8,128)(2,1)}, bf16[32,896]{1,0:T(8,128)(2,1)S(1)}, u32[]{:S(2)}, u32[]{:S(2)}) collective-permute-start(bf16[32,896]{1,0:T(8,128)(2,1)} %get-tuple-element.141), channel_id=1, source_target_pairs={{0,8},{1,9},{2,10},{3,11},{4,12},{5,13},{6,14},{7,15},{8,0},{9,1},... | collective-permute-start | bytes 172040 | tf_op jit(solution)/shard_map/ppermute | solution.py:922
  8.2 13.0 %collective-permute-start.2 = (bf16[32,896]{1,0:T(8,128)(2,1)}, bf16[32,896]{1,0:T(8,128)(2,1)S(1)}, u32[]{:S(2)}, u32[]{:S(2)}) collective-permute-start(bf16[32,896]{1,0:T(8,128)(2,1)} %get-tuple-element.141), channel_id=1, source_target_pairs={{0,12},{1,13},{2,14},{3,15},{4,8},{5,9},{6,10},{7,11},{8,4},{9,5},... | collective-permute-start | bytes 172040 | tf_op jit(solution)/shard_map/ppermute | solution.py:922
  8.2 34.4 %collective-permute-start.8 = (bf16[32,2304]{1,0:T(8,128)(2,1)}, bf16[32,2304]{1,0:T(8,128)(2,1)S(1)}, u32[]{:S(2)}, u32[]{:S(2)}) collective-permute-start(bf16[32,2304]{1,0:T(8,128)(2,1)} %get-tuple-element.151), channel_id=1, source_target_pairs={{0,4},{1,5},{2,6},{3,7},{4,0},{5,1},{6,2},{7,3},{8,12},{9,13},{10,... | collective-permute-start | bytes 442376 | tf_op jit(solution)/shard_map/ppermute | solution.py:922
  10.6 7.1 %copy-start.4 = (bf16[32,2304]{1,0:T(8,128)(2,1)S(1)}, bf16[32,2304]{1,0:T(8,128)(2,1)}, u32[]{:S(2)}) copy-start(bf16[32,2304]{1,0:T(8,128)(2,1)} %get-tuple-element.151) | copy-start | bytes 442372
  10.6 10.7 %copy-start.10 = (bf16[1,4,392,512]{3,2,1,0:T(8,128)(2,1)S(1)}, bf16[1,4,392,512]{3,2,1,0:T(8,128)(2,1)}, u32[]{:S(2)}) copy-start(bf16[1,4,392,512]{3,2,1,0:T(8,128)(2,1)} %param.40) | copy-start | bytes 4816900
  10.6 10.7 %copy-start.5 = (bf16[32,896]{1,0:T(8,128)(2,1)S(1)}, bf16[32,896]{1,0:T(8,128)(2,1)}, u32[]{:S(2)}) copy-start(bf16[32,896]{1,0:T(8,128)(2,1)} %get-tuple-element.141) | copy-start | bytes 172036
  17.7 24.8 %collective-permute-start.9 = (bf16[32,2304]{1,0:T(8,128)(2,1)S(1)}, bf16[32,2304]{1,0:T(8,128)(2,1)S(1)}, u32[]{:S(2)}, u32[]{:S(2)}) collective-permute-start(bf16[32,2304]{1,0:T(8,128)(2,1)S(1)} %copy-done.4), channel_id=1, source_target_pairs={{0,8},{1,9},{2,10},{3,11},{4,12},{5,13},{6,14},{7,15},{8,0},{9,1},... | collective-permute-start | bytes 442376 | tf_op jit(solution)/shard_map/ppermute | solution.py:922
  21.2 21.3 %collective-permute-start.10 = (bf16[32,2304]{1,0:T(8,128)(2,1)S(1)}, bf16[32,2304]{1,0:T(8,128)(2,1)S(1)}, u32[]{:S(2)}, u32[]{:S(2)}) collective-permute-start(bf16[32,2304]{1,0:T(8,128)(2,1)S(1)} %copy-done.4), channel_id=1, source_target_pairs={{0,12},{1,13},{2,14},{3,15},{4,8},{5,9},{6,10},{7,11},{8,4},{9,5},... | collective-permute-start | bytes 442376 | tf_op jit(solution)/shard_map/ppermute | solution.py:922
  21.3 15.6 %collective-permute-start.6 = (bf16[1,4,392,512]{3,2,1,0:T(8,128)(2,1)S(1)}, bf16[1,4,392,512]{3,2,1,0:T(8,128)(2,1)S(1)}, u32[]{:S(2)}, u32[]{:S(2)}) collective-permute-start(bf16[1,4,392,512]{3,2,1,0:T(8,128)(2,1)S(1)} %copy-done.10), channel_id=1, source_target_pairs={{0,16},{16,0},{1,17},{17,1},{2,18},{18,2},{3,19},{19,3},{4,20},{20... | collective-permute-start | bytes 4816904 | tf_op jit(solution)/shard_map/ppermute | solution.py:800
  21.4 7.5 %collective-permute-start.4 = (bf16[4,32,896]{2,1,0:T(8,128)(2,1)S(1)}, bf16[4,32,896]{2,1,0:T(8,128)(2,1)S(1)}, u32[]{:S(2)}, u32[]{:S(2)}) collective-permute-start(bf16[4,32,896]{2,1,0:T(8,128)(2,1)S(1)} %pad_maximum_fusion.3), channel_id=1, source_target_pairs={{0,2},{1,3},{2,0},{3,1},{4,6},{5,7},{6,4},{7,5},{8,10},{9,11},{10,... | collective-permute-start | bytes 688136 | tf_op jit(solution)/shard_map/ppermute | solution.py:922
  29.6 8.5 %collective-permute-start.5 = (bf16[8,32,896]{2,1,0:T(8,128)(2,1)S(1)}, bf16[8,32,896]{2,1,0:T(8,128)(2,1)S(1)}, u32[]{:S(2)}, u32[]{:S(2)}) collective-permute-start(bf16[8,32,896]{2,1,0:T(8,128)(2,1)S(1)} %get-tuple-element.281), channel_id=1, source_target_pairs={{0,1},{1,0},{2,3},{3,2},{4,5},{5,4},{6,7},{7,6},{8,9},{9,8},{10,11... | collective-permute-start | bytes 1376264 | tf_op jit(solution)/shard_map/ppermute | solution.py:922
  36.9 2.1 copy-start.11
  38.9 3.7 %collective-permute-start.7 = (bf16[16,32,896]{2,1,0:T(8,128)(2,1)}, bf16[16,32,896]{2,1,0:T(8,128)(2,1)S(1)}, u32[]{:S(2)}, u32[]{:S(2)}) collective-permute-start(bf16[16,32,896]{2,1,0:T(8,128)(2,1)} %constant_dynamic-update-slice_fusion.5.own_ref), channel_id=1, source_target_pairs={{0,16},{16,0},{1,17},{17,1},{2,18},{18,2},{3,19},{19,3},{4,20},{20... | collective-permute-start | bytes 2752520 | tf_op jit(solution)/shard_map/ppermute | solution.py:800
  42.6 0.9 copy-start.12
  43.6 10.2 %collective-permute-start.11 = (bf16[4,32,2304]{2,1,0:T(8,128)(2,1)S(1)}, bf16[4,32,2304]{2,1,0:T(8,128)(2,1)S(1)}, u32[]{:S(2)}, u32[]{:S(2)}) collective-permute-start(bf16[4,32,2304]{2,1,0:T(8,128)(2,1)S(1)} %pad_maximum_fusion), channel_id=1, source_target_pairs={{0,2},{1,3},{2,0},{3,1},{4,6},{5,7},{6,4},{7,5},{8,10},{9,11},{10,... | collective-permute-start | bytes 1769480 | tf_op jit(solution)/shard_map/ppermute | solution.py:922
  53.9 19.8 %collective-permute-start.12 = (bf16[8,32,2304]{2,1,0:T(8,128)(2,1)S(1)}, bf16[8,32,2304]{2,1,0:T(8,128)(2,1)S(1)}, u32[]{:S(2)}, u32[]{:S(2)}) collective-permute-start(bf16[8,32,2304]{2,1,0:T(8,128)(2,1)S(1)} %get-tuple-element.273), channel_id=1, source_target_pairs={{0,1},{1,0},{2,3},{3,2},{4,5},{5,4},{6,7},{7,6},{8,9},{9,8},{10,11... | collective-permute-start | bytes 3538952 | tf_op jit(solution)/shard_map/ppermute | solution.py:922
  73.7 13.4 %copy-start.8 = (bf16[16,32,2304]{2,1,0:T(8,128)(2,1)}, bf16[16,32,2304]{2,1,0:T(8,128)(2,1)S(1)}, u32[]{:S(2)}) copy-start(bf16[16,32,2304]{2,1,0:T(8,128)(2,1)S(1)} %constant_dynamic-update-slice_fusion.16.own_ref) | copy-start | bytes 7077892
  73.7 13.4 %collective-permute-start.13 = (bf16[16,32,2304]{2,1,0:T(8,128)(2,1)S(1)}, bf16[16,32,2304]{2,1,0:T(8,128)(2,1)S(1)}, u32[]{:S(2)}, u32[]{:S(2)}) collective-permute-start(bf16[16,32,2304]{2,1,0:T(8,128)(2,1)S(1)} %constant_dynamic-update-slice_fusion.16.own_ref), channel_id=1, source_target_pairs={{0,16},{16,0},{1,17},{17,1},{2,18},{18,2},{3,19},{19,3},{4,20},{20... | collective-permute-start | bytes 7077896 | tf_op jit(solution)/shard_map/ppermute | solution.py:800
  87.1 1.4 copy-start.9
  131.1 22.6 %collective-permute-start.14 = (bf16[16,32,2304]{2,1,0:T(8,128)(2,1)}, bf16[16,32,2304]{2,1,0:T(8,128)(2,1)S(1)}, u32[]{:S(2)}, u32[]{:S(2)}) collective-permute-start(bf16[16,32,2304]{2,1,0:T(8,128)(2,1)} %get-tuple-element.201), channel_id=1, source_target_pairs={{0,16},{16,0},{1,17},{17,1},{2,18},{18,2},{3,19},{19,3},{4,20},{20... | collective-permute-start | bytes 7077896 | tf_op jit(solution)/shard_map/ppermute | solution.py:800
  131.2 22.5 %copy-start.1 = (bf16[16,32,2304]{2,1,0:T(8,128)(2,1)S(1)}, bf16[16,32,2304]{2,1,0:T(8,128)(2,1)}, u32[]{:S(2)}) copy-start(bf16[16,32,2304]{2,1,0:T(8,128)(2,1)} %get-tuple-element.214) | copy-start | bytes 7077892
  154.4 0.9 copy-start.7
  154.5 23.2 %collective-permute-start.15 = (bf16[8,32,2304]{2,1,0:T(8,128)(2,1)S(1)}, bf16[8,32,2304]{2,1,0:T(8,128)(2,1)S(1)}, u32[]{:S(2)}, u32[]{:S(2)}) collective-permute-start(bf16[8,32,2304]{2,1,0:T(8,128)(2,1)S(1)} %slice.74), channel_id=1, source_target_pairs={{0,1},{1,0},{2,3},{3,2},{4,5},{5,4},{6,7},{7,6},{8,9},{9,8},{10,11... | collective-permute-start | bytes 3538952 | tf_op jit(solution)/shard_map/ppermute | solution.py:922
  177.7 1.9 copy-start.6
  178.0 17.7 %collective-permute-start.16 = (bf16[4,32,2304]{2,1,0:T(8,128)(2,1)S(1)}, bf16[4,32,2304]{2,1,0:T(8,128)(2,1)S(1)}, u32[]{:S(2)}, u32[]{:S(2)}) collective-permute-start(bf16[4,32,2304]{2,1,0:T(8,128)(2,1)S(1)} %slice.76), channel_id=1, source_target_pairs={{0,2},{1,3},{2,0},{3,1},{4,6},{5,7},{6,4},{7,5},{8,10},{9,11},{10,... | collective-permute-start | bytes 1769480 | tf_op jit(solution)/shard_map/ppermute | solution.py:922
  179.7 16.0 %collective-permute-start.17 = (bf16[16,2816]{1,0:T(8,128)(2,1)S(1)}, bf16[16,2816]{1,0:T(8,128)(2,1)S(1)}, u32[]{:S(2)}, u32[]{:S(2)}) collective-permute-start(bf16[16,2816]{1,0:T(8,128)(2,1)S(1)} %convert_element_type.151), channel_id=1, source_target_pairs={{0,16},{16,0},{1,17},{17,1},{2,18},{18,2},{3,19},{19,3},{4,20},{20... | collective-permute-start | bytes 270344 | tf_op jit(solution)/shard_map/ppermute | solution.py:989
  195.7 10.4 %collective-permute-start.18 = (bf16[16,32,896]{2,1,0:T(8,128)(2,1)}, bf16[16,32,896]{2,1,0:T(8,128)(2,1)S(1)}, u32[]{:S(2)}, u32[]{:S(2)}) collective-permute-start(bf16[16,32,896]{2,1,0:T(8,128)(2,1)} %get-tuple-element.229), channel_id=1, source_target_pairs={{0,16},{16,0},{1,17},{17,1},{2,18},{18,2},{3,19},{19,3},{4,20},{20... | collective-permute-start | bytes 2752520 | tf_op jit(solution)/shard_map/ppermute | solution.py:800
  196.3 9.8 %collective-permute-start.19 = (bf16[16,2816]{1,0:T(8,128)(2,1)S(1)}, bf16[16,2816]{1,0:T(8,128)(2,1)S(1)}, u32[]{:S(2)}, u32[]{:S(2)}) collective-permute-start(bf16[16,2816]{1,0:T(8,128)(2,1)S(1)} %add_convert_fusion.8), channel_id=1, source_target_pairs={{0,1},{1,0},{2,3},{3,2},{4,5},{5,4},{6,7},{7,6},{8,9},{9,8},{10,11... | collective-permute-start | bytes 270344 | tf_op jit(solution)/shard_map/ppermute | solution.py:989
  197.8 9.4 %collective-permute-start.22 = (bf16[32,2304]{1,0:T(8,128)(2,1)S(1)}, bf16[32,2304]{1,0:T(8,128)(2,1)S(1)}, u32[]{:S(2)}, u32[]{:S(2)}) collective-permute-start(bf16[32,2304]{1,0:T(8,128)(2,1)S(1)} %get-tuple-element.271), channel_id=1, source_target_pairs={{0,4},{1,5},{2,6},{3,7},{4,0},{5,1},{6,2},{7,3},{8,12},{9,13},{10,... | collective-permute-start | bytes 442376 | tf_op jit(solution)/shard_map/ppermute | solution.py:922
  198.3 14.8 %collective-permute-start.23 = (bf16[32,2304]{1,0:T(8,128)(2,1)S(1)}, bf16[32,2304]{1,0:T(8,128)(2,1)S(1)}, u32[]{:S(2)}, u32[]{:S(2)}) collective-permute-start(bf16[32,2304]{1,0:T(8,128)(2,1)S(1)} %get-tuple-element.270), channel_id=1, source_target_pairs={{0,8},{1,9},{2,10},{3,11},{4,12},{5,13},{6,14},{7,15},{8,0},{9,1},... | collective-permute-start | bytes 442376 | tf_op jit(solution)/shard_map/ppermute | solution.py:922
  202.1 4.0 %copy-start.3 = (bf16[16,32,896]{2,1,0:T(8,128)(2,1)S(1)}, bf16[16,32,896]{2,1,0:T(8,128)(2,1)}, u32[]{:S(2)}) copy-start(bf16[16,32,896]{2,1,0:T(8,128)(2,1)} %get-tuple-element.222) | copy-start | bytes 2752516
  202.1 11.0 %collective-permute-start.24 = (bf16[32,2304]{1,0:T(8,128)(2,1)S(1)}, bf16[32,2304]{1,0:T(8,128)(2,1)S(1)}, u32[]{:S(2)}, u32[]{:S(2)}) collective-permute-start(bf16[32,2304]{1,0:T(8,128)(2,1)S(1)} %get-tuple-element.269), channel_id=1, source_target_pairs={{0,12},{1,13},{2,14},{3,15},{4,8},{5,9},{6,10},{7,11},{8,4},{9,5},... | collective-permute-start | bytes 442376 | tf_op jit(solution)/shard_map/ppermute | solution.py:922
  206.1 1.2 copy-start.14
  206.4 8.5 %collective-permute-start.20 = (bf16[8,32,896]{2,1,0:T(8,128)(2,1)S(1)}, bf16[8,32,896]{2,1,0:T(8,128)(2,1)S(1)}, u32[]{:S(2)}, u32[]{:S(2)}) collective-permute-start(bf16[8,32,896]{2,1,0:T(8,128)(2,1)S(1)} %slice.78), channel_id=1, source_target_pairs={{0,1},{1,0},{2,3},{3,2},{4,5},{5,4},{6,7},{7,6},{8,9},{9,8},{10,11... | collective-permute-start | bytes 1376264 | tf_op jit(solution)/shard_map/ppermute | solution.py:922
  207.3 7.7 %collective-permute-start.25 = (bf16[4,208,512]{2,1,0:T(8,128)(2,1)S(1)}, bf16[4,208,512]{2,1,0:T(8,128)(2,1)S(1)}, u32[]{:S(2)}, u32[]{:S(2)}) collective-permute-start(bf16[4,208,512]{2,1,0:T(8,128)(2,1)S(1)} %copy-done.14), channel_id=1, source_target_pairs={{0,16},{16,0},{1,17},{17,1},{2,18},{18,2},{3,19},{19,3},{4,20},{20... | collective-permute-start | bytes 2555912 | tf_op jit(solution)/shard_map/ppermute | solution.py:800
  207.3 5.8 %collective-permute-start.21 = (bf16[16,2816]{1,0:T(8,128)(2,1)S(1)}, bf16[16,2816]{1,0:T(8,128)(2,1)S(1)}, u32[]{:S(2)}, u32[]{:S(2)}) collective-permute-start(bf16[16,2816]{1,0:T(8,128)(2,1)S(1)} %add_convert_fusion.7), channel_id=1, source_target_pairs={{0,2},{1,3},{2,0},{3,1},{4,6},{5,7},{6,4},{7,5},{8,10},{9,11},{10,... | collective-permute-start | bytes 270344 | tf_op jit(solution)/shard_map/ppermute | solution.py:989
  207.9 13.0 %copy-start = (f32[4,392,512]{2,1,0:T(8,128)S(1)}, f32[4,392,512]{2,1,0:T(8,128)}, u32[]{:S(2)}) copy-start(f32[4,392,512]{2,1,0:T(8,128)} %get-tuple-element.245) | copy-start | bytes 9633796
  211.4 8.7 %copy-start.13 = (bf16[4,208,512]{2,1,0:T(8,128)(2,1)S(1)}, bf16[4,208,512]{2,1,0:T(8,128)(2,1)}, u32[]{:S(2)}) copy-start(bf16[4,208,512]{2,1,0:T(8,128)(2,1)} %get-tuple-element.249) | copy-start | bytes 2555908
  215.0 5.3 %collective-permute-start.27 = (bf16[16,2816]{1,0:T(8,128)(2,1)S(1)}, bf16[16,2816]{1,0:T(8,128)(2,1)S(1)}, u32[]{:S(2)}, u32[]{:S(2)}) collective-permute-start(bf16[16,2816]{1,0:T(8,128)(2,1)S(1)} %add_convert_fusion.6), channel_id=1, source_target_pairs={{0,4},{1,5},{2,6},{3,7},{4,0},{5,1},{6,2},{7,3},{8,12},{9,13},{10,... | collective-permute-start | bytes 270344 | tf_op jit(solution)/shard_map/ppermute | solution.py:922
  215.8 10.6 %collective-permute-start.28 = (bf16[16,2816]{1,0:T(8,128)(2,1)S(1)}, bf16[16,2816]{1,0:T(8,128)(2,1)S(1)}, u32[]{:S(2)}, u32[]{:S(2)}) collective-permute-start(bf16[16,2816]{1,0:T(8,128)(2,1)S(1)} %add_convert_fusion.6), channel_id=1, source_target_pairs={{0,8},{1,9},{2,10},{3,11},{4,12},{5,13},{6,14},{7,15},{8,0},{9,1},... | collective-permute-start | bytes 270344 | tf_op jit(solution)/shard_map/ppermute | solution.py:922
  219.2 7.2 %collective-permute-start.29 = (bf16[16,2816]{1,0:T(8,128)(2,1)S(1)}, bf16[16,2816]{1,0:T(8,128)(2,1)S(1)}, u32[]{:S(2)}, u32[]{:S(2)}) collective-permute-start(bf16[16,2816]{1,0:T(8,128)(2,1)S(1)} %add_convert_fusion.6), channel_id=1, source_target_pairs={{0,12},{1,13},{2,14},{3,15},{4,8},{5,9},{6,10},{7,11},{8,4},{9,5},... | collective-permute-start | bytes 270344 | tf_op jit(solution)/shard_map/ppermute | solution.py:922
  219.6 6.8 %collective-permute-start.26 = (bf16[4,32,896]{2,1,0:T(8,128)(2,1)S(1)}, bf16[4,32,896]{2,1,0:T(8,128)(2,1)S(1)}, u32[]{:S(2)}, u32[]{:S(2)}) collective-permute-start(bf16[4,32,896]{2,1,0:T(8,128)(2,1)S(1)} %slice.84), channel_id=1, source_target_pairs={{0,2},{1,3},{2,0},{3,1},{4,6},{5,7},{6,4},{7,5},{8,10},{9,11},{10,... | collective-permute-start | bytes 688136 | tf_op jit(solution)/shard_map/ppermute | solution.py:922
  220.2 6.2 %collective-permute-start.31 = (bf16[4,208,512]{2,1,0:T(8,128)(2,1)S(1)}, bf16[4,208,512]{2,1,0:T(8,128)(2,1)S(1)}, u32[]{:S(2)}, u32[]{:S(2)}) collective-permute-start(bf16[4,208,512]{2,1,0:T(8,128)(2,1)S(1)} %copy-done.13), channel_id=1, source_target_pairs={{0,16},{16,0},{1,17},{17,1},{2,18},{18,2},{3,19},{19,3},{4,20},{20... | collective-permute-start | bytes 2555912 | tf_op jit(solution)/shard_map/ppermute | solution.py:800
  220.2 6.1 %collective-permute-start.30 = (bf16[32,2304]{1,0:T(8,128)(2,1)S(1)}, bf16[32,2304]{1,0:T(8,128)(2,1)S(1)}, u32[]{:S(2)}, u32[]{:S(2)}) collective-permute-start(bf16[32,2304]{1,0:T(8,128)(2,1)S(1)} %fusion.7), channel_id=1, source_target_pairs={{0,16},{16,0},{1,17},{17,1},{2,18},{18,2},{3,19},{19,3},{4,20},{20... | collective-permute-start | bytes 442376 | tf_op jit(solution)/shard_map/ppermute | solution.py:800
  222.8 8.3 %copy-start.2 = (bf16[4,392,512]{2,1,0:T(8,128)(2,1)S(1)}, bf16[4,392,512]{2,1,0:T(8,128)(2,1)}, u32[]{:S(2)}) copy-start(bf16[4,392,512]{2,1,0:T(8,128)(2,1)} %get-tuple-element.252) | copy-start | bytes 4816900
  226.6 14.3 %collective-permute-start.32 = (bf16[32,896]{1,0:T(8,128)(2,1)S(1)}, bf16[32,896]{1,0:T(8,128)(2,1)S(1)}, u32[]{:S(2)}, u32[]{:S(2)}) collective-permute-start(bf16[32,896]{1,0:T(8,128)(2,1)S(1)} %get-tuple-element.280), channel_id=1, source_target_pairs={{0,4},{1,5},{2,6},{3,7},{4,0},{5,1},{6,2},{7,3},{8,12},{9,13},{10,... | collective-permute-start | bytes 172040 | tf_op jit(solution)/shard_map/ppermute | solution.py:922
  228.4 12.6 %collective-permute-start.33 = (bf16[32,896]{1,0:T(8,128)(2,1)S(1)}, bf16[32,896]{1,0:T(8,128)(2,1)S(1)}, u32[]{:S(2)}, u32[]{:S(2)}) collective-permute-start(bf16[32,896]{1,0:T(8,128)(2,1)S(1)} %get-tuple-element.279), channel_id=1, source_target_pairs={{0,8},{1,9},{2,10},{3,11},{4,12},{5,13},{6,14},{7,15},{8,0},{9,1},... | collective-permute-start | bytes 172040 | tf_op jit(solution)/shard_map/ppermute | solution.py:922
  230.1 10.8 %collective-permute-start.34 = (bf16[32,896]{1,0:T(8,128)(2,1)S(1)}, bf16[32,896]{1,0:T(8,128)(2,1)S(1)}, u32[]{:S(2)}, u32[]{:S(2)}) collective-permute-start(bf16[32,896]{1,0:T(8,128)(2,1)S(1)} %get-tuple-element.278), channel_id=1, source_target_pairs={{0,12},{1,13},{2,14},{3,15},{4,8},{5,9},{6,10},{7,11},{8,4},{9,5},... | collective-permute-start | bytes 172040 | tf_op jit(solution)/shard_map/ppermute | solution.py:922
  241.6 1.2 collective-permute-start.35
where the time goes:
time: 249 us; the launch traced here: 244 us
  Pallas kernels  179 us (72%)
  starting transfers between devices  35.7 us (14%)
  local copies, waits for them, and re-layouts  10.3 us (4%)
  other arithmetic  8.97 us (4%)
  waiting for transfers between devices  8.44 us (3%)
    pallas_call x2, Pallas kernels, attend_back(): pl.pallas_call(back_kernel, grid=(2, nw), in_specs=[pl.BlockSpec((1, GROU...  44.9 us
    pallas_call x1, Pallas kernels, feed(): pl.pallas_call(feed_kernel, grid_spec=pltpu.PrefetchScalarGridSpec(num_sc...  42.6 us
    ppermute x23, starting transfers between devices, hop(): return lax.ppermute(part, ('seq', 'shard'), pairs)  31.9 us
    pallas_call x2, Pallas kernels, attend(): pl.pallas_call(attend_kernel, grid=(nw,), in_specs=[pl.BlockSpec((1, half...  25.7 us
    pallas_call x1, Pallas kernels, input_side(): pl.pallas_call(input_kernel, grid_spec=pltpu.PrefetchScalarGridSpec(num_s...  15.9 us
    pallas_call x2, Pallas kernels, bias_half(): pl.pallas_call(bias_kernel, grid=(1,), in_specs=[pl.BlockSpec((8 * heads,...  11.6 us
    pallas_call x1, Pallas kernels, project(): pl.pallas_call(project_kernel, grid_spec=pltpu.PrefetchScalarGridSpec(num...  9.49 us
    ppermute x23, waiting for transfers between devices, hop(): return lax.ppermute(part, ('seq', 'shard'), pairs)  8.28 us
  transfers between devices with their start and end apart: 36, of which 5 were waited for; matrix products, arithmetic and copies ran while one was open for 6% of the time, Pallas kernels for 56%

commit v1 on v0

--- a/solution.py
+++ b/solution.py
@@ -21,7 +21,7 @@
 SCALE=HEAD_DIM**-0.5
 BIG=-(2.0**30)
 GROUP=4
-VM=56*1024*1024
+VM=54*1024*1024
 
 def cost(micros):
     return pl.CostEstimate(flops=int(micros * 1e9), bytes_accessed=int(micros * 3.6e6), transcendentals=0)

time: 249 us -> 245 us (0.984)
  local copies, waits for them, and re-layouts: 10.3 us -> 5.4 us
    unnamed x39, local copies, waits for them, and re-layouts: 6.09 us -> 2.62 us
  transfers between devices with their start and end apart: 36 -> 36, of which waited for: 5 -> 6; matrix products, arithmetic and copies ran while one was open for 6% -> 4% of each run, Pallas kernels for 56% -> 57%
where the time goes in v1:
time: 245 us; the launch traced here: 240 us
  Pallas kernels  179 us (73%)
  starting transfers between devices  38.1 us (16%)
  other arithmetic  8.99 us (4%)
  waiting for transfers between devices  7.15 us (3%)
  local copies, waits for them, and re-layouts  5.4 us (2%)
    pallas_call x2, Pallas kernels, attend_back(): pl.pallas_call(back_kernel, grid=(2, nw), in_specs=[pl.BlockSpec((1, GROU...  44.9 us
    pallas_call x1, Pallas kernels, feed(): pl.pallas_call(feed_kernel, grid_spec=pltpu.PrefetchScalarGridSpec(num_sc...  42.6 us
    ppermute x23, starting transfers between devices, hop(): return lax.ppermute(part, ('seq', 'shard'), pairs)  33.3 us
    pallas_call x2, Pallas kernels, attend(): pl.pallas_call(attend_kernel, grid=(nw,), in_specs=[pl.BlockSpec((1, half...  25.7 us
    pallas_call x1, Pallas kernels, input_side(): pl.pallas_call(input_kernel, grid_spec=pltpu.PrefetchScalarGridSpec(num_s...  15.9 us
    pallas_call x2, Pallas kernels, bias_half(): pl.pallas_call(bias_kernel, grid=(1,), in_specs=[pl.BlockSpec((8 * heads,...  11.6 us
    pallas_call x1, Pallas kernels, project(): pl.pallas_call(project_kernel, grid_spec=pltpu.PrefetchScalarGridSpec(num...  9.49 us
    pallas_call x2, Pallas kernels, enter(): pl.pallas_call(enter_kernel, grid=(2,), in_specs=[part, part, pl.BlockSpe...  7.67 us
  transfers between devices with their start and end apart: 36, of which 6 were waited for; matrix products, arithmetic and copies ran while one was open for 4% of the time, Pallas kernels for 57%

profile of v1, /device:TPU:0, one launch (start us, length us, event | category | flops | bytes accessed | tf_op | source)
XLA Modules:
  0.0 240.1 jit_solution(2746923095341946919)
XLA Ops:
  0.7 0.5 collective-permute-start.3
  1.2 1.9 pack.1
  3.0 2.6 %collective-permute-start = (bf16[32,896]{1,0:T(8,128)(2,1)}, bf16[32,896]{1,0:T(8,128)(2,1)S(1)}, u32[]{:S(2)}, u32[]{:S(2)}) collective-permute-start(bf16[32,896]{1,0:T(8,128)(2,1)} %get-tuple-element.141), channel_id=1, source_target_pairs={{0,4},{1,5},{2,6},{3,7},{4,0},{5,1},{6,2},{7,3},{8,12},{9,13},{10,... | collective-permute-start | bytes 172040 | tf_op jit(solution)/shard_map/ppermute | solution.py:922
  5.6 2.6 %collective-permute-start.1 = (bf16[32,896]{1,0:T(8,128)(2,1)}, bf16[32,896]{1,0:T(8,128)(2,1)S(1)}, u32[]{:S(2)}, u32[]{:S(2)}) collective-permute-start(bf16[32,896]{1,0:T(8,128)(2,1)} %get-tuple-element.141), channel_id=1, source_target_pairs={{0,8},{1,9},{2,10},{3,11},{4,12},{5,13},{6,14},{7,15},{8,0},{9,1},... | collective-permute-start | bytes 172040 | tf_op jit(solution)/shard_map/ppermute | solution.py:922
  8.2 0.9 collective-permute-start.8
  9.1 0.8 constant_dynamic-update-slice_fusion.4
  10.0 6.4 %prepare.1 = (s32[2,2816]{1,0:T(2,128)}, f32[128,1408]{1,0:T(8,128)}, bf16[4,392,128]{2,1,0:T(8,128)(2,1)}, bf16[4,32,392]{2,1,0:T(8,128)(2,1)}) custom-call(s32[392,392]{1,0:T(8,128)} %rel_ref.1, s32[4,2816]{1,0:T(4,128)} %constant.116.clone.maps_ref, bf16[16,2535]{1,0:T(8,128)(2,1)} %bitcast.85, s32[4,392]{1,0:T(4,128)} %region_ref.1, ...), custom_call_target="tpu_custom_call" | custom-call | flops 6000000000 | bytes 21600000 | tf_op jit(solution)/shard_map/prepare/pallas_call | solution.py:312
  16.4 0.6 concatenate.35.places_ref
  17.1 3.5 %collective-permute-start.9 = (bf16[32,2304]{1,0:T(8,128)(2,1)S(1)}, bf16[32,2304]{1,0:T(8,128)(2,1)S(1)}, u32[]{:S(2)}, u32[]{:S(2)}) collective-permute-start(bf16[32,2304]{1,0:T(8,128)(2,1)S(1)} %copy-done.4), channel_id=1, source_target_pairs={{0,8},{1,9},{2,10},{3,11},{4,12},{5,13},{6,14},{7,15},{8,0},{9,1},... | collective-permute-start | bytes 442376 | tf_op jit(solution)/shard_map/ppermute | solution.py:922
  20.7 1.7 collective-permute-start.4
  22.4 3.9 %enter.2.x_ref = bf16[4,392,512]{2,1,0:T(8,128)(2,1)} custom-call(bf16[4,392,512]{2,1,0:T(8,128)(2,1)} %bitcast.81, bf16[4,392,512]{2,1,0:T(8,128)(2,1)} %bitcast.9.arrived_ref, bf16[392,392]{1,0:T(8,128)(2,1)} %constant.111.clone.order_ref), custom_call_target="tpu_custom_call" | custom-call | flops 4000000000 | bytes 14400000 | tf_op jit(solution)/shard_map/enter/pallas_call | solution.py:836
  26.4 0.4 collective-permute-done.4
  26.8 1.7 collective-permute-start.5
  28.5 5.8 %position_bias.2.bias_ref = bf16[8,392,392]{2,1,0:T(8,128)(2,1)} custom-call(f32[128,1408]{1,0:T(8,128)} %get-tuple-element.178.narrow_ref, s32[392,128]{1,0:T(8,128)} %constant.113.clone.spot_ref), custom_call_target="tpu_custom_call" | custom-call | flops 5000000000 | bytes 18000000 | tf_op jit(solution)/shard_map/position_bias/pallas_call | solution.py:354
  34.3 1.1 collective-permute-done.5
  35.6 3.8 %enter.3.og_ref = bf16[4,392,512]{2,1,0:T(8,128)(2,1)} custom-call(bf16[4,392,512]{2,1,0:T(8,128)(2,1)} %bitcast.82, bf16[4,392,512]{2,1,0:T(8,128)(2,1)} %bitcast.83, bf16[392,392]{1,0:T(8,128)(2,1)} %constant.111.clone.order_ref), custom_call_target="tpu_custom_call" | custom-call | flops 4000000000 | bytes 14400000 | tf_op jit(solution)/shard_map/enter/pallas_call | solution.py:836
  39.5 1.7 collective-permute-start.11
  41.3 9.5 %project.1 = (bf16[4,512,392]{2,1,0:T(8,128)(2,1)}, bf16[4,512,392]{2,1,0:T(8,128)(2,1)}, bf16[4,512,392]{2,1,0:T(8,128)(2,1)}, bf16[4,392,512]{2,1,0:T(8,128)(2...) custom-call(s32[65]{0:T(128)} %concatenate.35.places_ref, bf16[4,392,512]{2,1,0:T(8,128)(2,1)} %enter.2.x_ref, ...), custom_call_target="tpu_custom_call" | custom-call | flops 8999999488 | bytes 32400000 | tf_op jit(solution)/shard_map/project/pallas_call | solution.py:468
  50.9 1.6 collective-permute-start.12
  52.5 12.5 %attend.2 = (bf16[4,256,392]{2,1,0:T(8,128)(2,1)}, bf16[4,392,256]{2,1,0:T(8,128)(2,1)}, bf16[4,8,392,392]{3,2,1,0:T(8,128)(2,1)}, f32[4,8,392]{2,1,0:T(8,128)}) custom-call(bf16[4,512,392]{2,1,0:T(8,128)(2,1)} %get-tuple-element.182.q_ref, bf16[4,392,512]{2,1,0:T(8,128)(2,1)} %get-tuple-element.164.k_ref, bf16[4,512,392]{2,1,0:T(8,128)(2,1)} %get-tuple-element.165.v_ref, ...), custom_call_target="tpu_custom_call" | custom-call | flops 10000000000 | bytes 36000000 | tf_op jit(solution)/shard_map/attend/pallas_call | solution.py:105
  64.9 5.8 %position_bias.3.bias_ref = bf16[8,392,392]{2,1,0:T(8,128)(2,1)} custom-call(f32[128,1408]{1,0:T(8,128)} %get-tuple-element.178.narrow_ref, s32[392,128]{1,0:T(8,128)} %constant.113.clone.spot_ref), custom_call_target="tpu_custom_call" | custom-call | flops 5000000000 | bytes 18000000 | tf_op jit(solution)/shard_map/position_bias/pallas_call | solution.py:354
  70.9 13.3 %attend.3 = (bf16[4,256,392]{2,1,0:T(8,128)(2,1)}, bf16[4,392,256]{2,1,0:T(8,128)(2,1)}, bf16[4,8,392,392]{3,2,1,0:T(8,128)(2,1)}, f32[4,8,392]{2,1,0:T(8,128)}) custom-call(bf16[4,512,392]{2,1,0:T(8,128)(2,1)} %get-tuple-element.182.q_ref, bf16[4,392,512]{2,1,0:T(8,128)(2,1)} %get-tuple-element.164.k_ref, bf16[4,512,392]{2,1,0:T(8,128)(2,1)} %get-tuple-element.165.v_ref, ...), custom_call_target="tpu_custom_call" | custom-call | flops 10000000000 | bytes 36000000 | tf_op jit(solution)/shard_map/attend/pallas_call | solution.py:105
  84.2 1.4 copy-done.10
  85.6 42.6 %feed_forward.1 = (bf16[4,392,512]{2,1,0:T(8,128)(2,1)}, f32[4,392,512]{2,1,0:T(8,128)}, bf16[4,512,392]{2,1,0:T(8,128)(2,1)}, bf16[16,32,2304]{2,1,0:T(8,128)(2...) custom-call(s32[65]{0:T(128)} %concatenate.35.places_ref, bf16[4,392,512]{2,1,0:T(8,128)(2,1)} %enter.2.x_ref, ...), custom_call_target="tpu_custom_call" | custom-call | flops 44000002048 | bytes 158400000 | tf_op jit(solution)/shard_map/feed_forward/pallas_call | solution.py:596
  128.3 22.5 %attend_back.2 = (bf16[4,392,256]{2,1,0:T(8,128)(2,1)}, bf16[4,392,256]{2,1,0:T(8,128)(2,1)}, bf16[4,392,256]{2,1,0:T(8,128)(2,1)}, f32[2,4,2816]{2,1,0:T(4,128)}) custom-call(bf16[4,8,392,392]{3,2,1,0:T(8,128)(2,1)} %get-tuple-element.179.e_ref, bf16[4,512,392]{2,1,0:T(8,128)(2,1)} %get-tuple-element.180.k_ref, ...), custom_call_target="tpu_custom_call" | custom-call | flops 20000000000 | bytes 72000000 | tf_op jit(solution)/shard_map/attend_back/pallas_call | solution.py:234
  150.8 0.6 add_convert_fusion
  151.5 0.7 collective-permute-start.15
  152.4 22.4 %attend_back.3 = (bf16[4,392,256]{2,1,0:T(8,128)(2,1)}, bf16[4,392,256]{2,1,0:T(8,128)(2,1)}, bf16[4,392,256]{2,1,0:T(8,128)(2,1)}, f32[2,4,2816]{2,1,0:T(4,128)}) custom-call(bf16[4,8,392,392]{3,2,1,0:T(8,128)(2,1)} %get-tuple-element.206.e_ref, bf16[4,512,392]{2,1,0:T(8,128)(2,1)} %get-tuple-element.180.k_ref, ...), custom_call_target="tpu_custom_call" | custom-call | flops 20000000000 | bytes 72000000 | tf_op jit(solution)/shard_map/attend_back/pallas_call | solution.py:234
  174.7 0.3 add_convert_fusion.1
  175.1 0.8 collective-permute-start.16
  176.0 0.3 collective-permute-start.17
  176.3 15.9 %input_side.1 = (bf16[4,392,512]{2,1,0:T(8,128)(2,1)}, bf16[16,32,896]{2,1,0:T(8,128)(2,1)}, bf16[16,32,896]{2,1,0:T(8,128)(2,1)}) custom-call(s32[65]{0:T(128)} %concatenate.35.places_ref, bf16[4,392,512]{2,1,0:T(8,128)(2,1)} %enter.2.x_ref, bf16[4,392,256]{2,1,0:T(8,128)(2,1)} %get-tuple-element.203.dq0, bf16[4,392,256]{2,1,0:T(8,128)(2,1)} %get-tuple-element.204.dk0, ...), custom_call_target="tpu_custom_call" | custom-call | flops 15000000512 | bytes 54000000 | tf_op jit(solution)/shard_map/input_side/pallas_call | solution.py:690
  192.2 0.3 collective-permute-start.18
  192.5 1.4 collective-permute-start.19
  194.1 0.5 collective-permute-start.22
  194.6 3.8 %collective-permute-start.23 = (bf16[32,2304]{1,0:T(8,128)(2,1)S(1)}, bf16[32,2304]{1,0:T(8,128)(2,1)S(1)}, u32[]{:S(2)}, u32[]{:S(2)}) collective-permute-start(bf16[32,2304]{1,0:T(8,128)(2,1)S(1)} %get-tuple-element.270), channel_id=1, source_target_pairs={{0,8},{1,9},{2,10},{3,11},{4,12},{5,13},{6,14},{7,15},{8,0},{9,1},... | collective-permute-start | bytes 442376 | tf_op jit(solution)/shard_map/ppermute | solution.py:922
  198.3 0.2 collective-permute-start.24
  198.5 3.8 %leave.2 = (f32[4,392,512]{2,1,0:T(8,128)}, bf16[4,208,512]{2,1,0:T(8,128)(2,1)}) custom-call(bf16[4,392,512]{2,1,0:T(8,128)(2,1)} %get-tuple-element.231.rows_ref, bf16[392,392]{1,0:T(8,128)(2,1)} %constant.124.order_ref), custom_call_target="tpu_custom_call" | custom-call | flops 4000000000 | bytes 14400000 | tf_op jit(solution)/shard_map/leave/pallas_call | solution.py:855
  202.4 0.2 add_convert_fusion.2
  202.6 0.8 collective-permute-start.20
  203.5 1.4 collective-permute-start.21
  204.9 3.6 %leave.3 = (bf16[4,392,512]{2,1,0:T(8,128)(2,1)}, bf16[4,208,512]{2,1,0:T(8,128)(2,1)}) custom-call(bf16[4,392,512]{2,1,0:T(8,128)(2,1)} %get-tuple-element.239.rows_ref, bf16[392,392]{1,0:T(8,128)(2,1)} %constant.124.order_ref), custom_call_target="tpu_custom_call" | custom-call | flops 4000000000 | bytes 14400000 | tf_op jit(solution)/shard_map/leave/pallas_call | solution.py:855
  208.5 0.9 collective-permute-done.23
  209.4 1.8 collective-permute-done.20
  211.2 1.0 collective-permute-start.27
  212.2 3.2 %collective-permute-start.28 = (bf16[16,2816]{1,0:T(8,128)(2,1)S(1)}, bf16[16,2816]{1,0:T(8,128)(2,1)S(1)}, u32[]{:S(2)}, u32[]{:S(2)}) collective-permute-start(bf16[16,2816]{1,0:T(8,128)(2,1)S(1)} %add_convert_fusion.6), channel_id=1, source_target_pairs={{0,8},{1,9},{2,10},{3,11},{4,12},{5,13},{6,14},{7,15},{8,0},{9,1},... | collective-permute-start | bytes 270344 | tf_op jit(solution)/shard_map/ppermute | solution.py:922
  215.4 0.3 collective-permute-start.29
  215.8 1.4 collective-permute-start.26
  217.3 0.6 collective-permute-start.30
  217.9 2.0 select_bitcast_fusion
  219.9 2.7 %collective-permute-done.28 = bf16[16,2816]{1,0:T(8,128)(2,1)S(1)} collective-permute-done((bf16[16,2816]{1,0:T(8,128)(2,1)S(1)}, bf16[16,2816]{1,0:T(8,128)(2,1)S(1)}, u32[]{:S(2)}, u32[]{:S(2)}) %collective-permute-start.28) | collective-permute-done | bytes 90144 | tf_op jit(solution)/shard_map/ppermute | solution.py:922
  222.9 1.8 collective-permute-start.32
  224.7 1.6 collective-permute-start.33
  226.4 1.0 collective-permute-start.34
  227.4 1.6 select_bitcast_fusion.1
  228.9 0.7 pad_maximum_fusion.1
  229.7 0.7 pad_maximum_fusion.2
  230.4 0.7 add_add_fusion.g_ref
  231.1 5.5 %table_rows.1 = f32[16,2535]{1,0:T(8,128)} custom-call(s32[2,2816]{1,0:T(2,128)} %get-tuple-element.254.lab_ref, f32[16,2816]{1,0:T(8,128)} %add_add_fusion.g_ref), custom_call_target="tpu_custom_call" | custom-call | flops 5000000000 | bytes 18000000 | tf_op jit(solution)/shard_map/table_rows/pallas_call | solution.py:380
  236.6 0.6 pad_maximum_fusion.6
  237.3 0.6 fusion.10
  237.9 0.5 slice_bitcast_fusion.9
  238.4 0.6 split.52
  239.2 0.7 pad_maximum_fusion.4
  (111 shorter events, 2.3 us)
Async XLA Ops:
  0.7 20.0 %collective-permute-start.3 = (bf16[1,4,392,512]{3,2,1,0:T(8,128)(2,1)}, bf16[1,4,392,512]{3,2,1,0:T(8,128)(2,1)}, u32[]{:S(2)}, u32[]{:S(2)}) collective-permute-start(bf16[1,4,392,512]{3,2,1,0:T(8,128)(2,1)} %param.24), channel_id=1, source_target_pairs={{0,16},{16,0},{1,17},{17,1},{2,18},{18,2},{3,19},{19,3},{4,20},{20... | collective-permute-start | bytes 4816904 | tf_op jit(solution)/shard_map/ppermute | solution.py:800
  3.0 14.0 %collective-permute-start = (bf16[32,896]{1,0:T(8,128)(2,1)}, bf16[32,896]{1,0:T(8,128)(2,1)S(1)}, u32[]{:S(2)}, u32[]{:S(2)}) collective-permute-start(bf16[32,896]{1,0:T(8,128)(2,1)} %get-tuple-element.141), channel_id=1, source_target_pairs={{0,4},{1,5},{2,6},{3,7},{4,0},{5,1},{6,2},{7,3},{8,12},{9,13},{10,... | collective-permute-start | bytes 172040 | tf_op jit(solution)/shard_map/ppermute | solution.py:922
  5.6 14.9 %collective-permute-start.1 = (bf16[32,896]{1,0:T(8,128)(2,1)}, bf16[32,896]{1,0:T(8,128)(2,1)S(1)}, u32[]{:S(2)}, u32[]{:S(2)}) collective-permute-start(bf16[32,896]{1,0:T(8,128)(2,1)} %get-tuple-element.141), channel_id=1, source_target_pairs={{0,8},{1,9},{2,10},{3,11},{4,12},{5,13},{6,14},{7,15},{8,0},{9,1},... | collective-permute-start | bytes 172040 | tf_op jit(solution)/shard_map/ppermute | solution.py:922
  8.2 12.3 %collective-permute-start.2 = (bf16[32,896]{1,0:T(8,128)(2,1)}, bf16[32,896]{1,0:T(8,128)(2,1)S(1)}, u32[]{:S(2)}, u32[]{:S(2)}) collective-permute-start(bf16[32,896]{1,0:T(8,128)(2,1)} %get-tuple-element.141), channel_id=1, source_target_pairs={{0,12},{1,13},{2,14},{3,15},{4,8},{5,9},{6,10},{7,11},{8,4},{9,5},... | collective-permute-start | bytes 172040 | tf_op jit(solution)/shard_map/ppermute | solution.py:922
  8.2 31.2 %collective-permute-start.8 = (bf16[32,2304]{1,0:T(8,128)(2,1)}, bf16[32,2304]{1,0:T(8,128)(2,1)S(1)}, u32[]{:S(2)}, u32[]{:S(2)}) collective-permute-start(bf16[32,2304]{1,0:T(8,128)(2,1)} %get-tuple-element.151), channel_id=1, source_target_pairs={{0,4},{1,5},{2,6},{3,7},{4,0},{5,1},{6,2},{7,3},{8,12},{9,13},{10,... | collective-permute-start | bytes 442376 | tf_op jit(solution)/shard_map/ppermute | solution.py:922
  10.0 7.1 %copy-start.4 = (bf16[32,2304]{1,0:T(8,128)(2,1)S(1)}, bf16[32,2304]{1,0:T(8,128)(2,1)}, u32[]{:S(2)}) copy-start(bf16[32,2304]{1,0:T(8,128)(2,1)} %get-tuple-element.151) | copy-start | bytes 442372
  10.0 10.7 %copy-start.5 = (bf16[32,896]{1,0:T(8,128)(2,1)S(1)}, bf16[32,896]{1,0:T(8,128)(2,1)}, u32[]{:S(2)}) copy-start(bf16[32,896]{1,0:T(8,128)(2,1)} %get-tuple-element.141) | copy-start | bytes 172036
  17.1 22.3 %collective-permute-start.9 = (bf16[32,2304]{1,0:T(8,128)(2,1)S(1)}, bf16[32,2304]{1,0:T(8,128)(2,1)S(1)}, u32[]{:S(2)}, u32[]{:S(2)}) collective-permute-start(bf16[32,2304]{1,0:T(8,128)(2,1)S(1)} %copy-done.4), channel_id=1, source_target_pairs={{0,8},{1,9},{2,10},{3,11},{4,12},{5,13},{6,14},{7,15},{8,0},{9,1},... | collective-permute-start | bytes 442376 | tf_op jit(solution)/shard_map/ppermute | solution.py:922
  20.5 18.8 %collective-permute-start.10 = (bf16[32,2304]{1,0:T(8,128)(2,1)S(1)}, bf16[32,2304]{1,0:T(8,128)(2,1)S(1)}, u32[]{:S(2)}, u32[]{:S(2)}) collective-permute-start(bf16[32,2304]{1,0:T(8,128)(2,1)S(1)} %copy-done.4), channel_id=1, source_target_pairs={{0,12},{1,13},{2,14},{3,15},{4,8},{5,9},{6,10},{7,11},{8,4},{9,5},... | collective-permute-start | bytes 442376 | tf_op jit(solution)/shard_map/ppermute | solution.py:922
  20.6 13.8 %collective-permute-start.6 = (bf16[1,4,392,512]{3,2,1,0:T(8,128)(2,1)}, bf16[1,4,392,512]{3,2,1,0:T(8,128)(2,1)S(1)}, u32[]{:S(2)}, u32[]{:S(2)}) collective-permute-start(bf16[1,4,392,512]{3,2,1,0:T(8,128)(2,1)} %param.40), channel_id=1, source_target_pairs={{0,16},{16,0},{1,17},{17,1},{2,18},{18,2},{3,19},{19,3},{4,20},{20... | collective-permute-start | bytes 4816904 | tf_op jit(solution)/shard_map/ppermute | solution.py:800
  20.7 6.1 %collective-permute-start.4 = (bf16[4,32,896]{2,1,0:T(8,128)(2,1)S(1)}, bf16[4,32,896]{2,1,0:T(8,128)(2,1)S(1)}, u32[]{:S(2)}, u32[]{:S(2)}) collective-permute-start(bf16[4,32,896]{2,1,0:T(8,128)(2,1)S(1)} %pad_maximum_fusion.3), channel_id=1, source_target_pairs={{0,2},{1,3},{2,0},{3,1},{4,6},{5,7},{6,4},{7,5},{8,10},{9,11},{10,... | collective-permute-start | bytes 688136 | tf_op jit(solution)/shard_map/ppermute | solution.py:922
  26.8 8.5 %collective-permute-start.5 = (bf16[8,32,896]{2,1,0:T(8,128)(2,1)S(1)}, bf16[8,32,896]{2,1,0:T(8,128)(2,1)S(1)}, u32[]{:S(2)}, u32[]{:S(2)}) collective-permute-start(bf16[8,32,896]{2,1,0:T(8,128)(2,1)S(1)} %get-tuple-element.281), channel_id=1, source_target_pairs={{0,1},{1,0},{2,3},{3,2},{4,5},{5,4},{6,7},{7,6},{8,9},{9,8},{10,11... | collective-permute-start | bytes 1376264 | tf_op jit(solution)/shard_map/ppermute | solution.py:922
  34.3 1.3 copy-start.11
  35.4 3.9 %copy-start.9 = (bf16[16,32,896]{2,1,0:T(8,128)(2,1)}, bf16[16,32,896]{2,1,0:T(8,128)(2,1)S(1)}, u32[]{:S(2)}) copy-start(bf16[16,32,896]{2,1,0:T(8,128)(2,1)S(1)} %constant_dynamic-update-slice_fusion.5.own_ref) | copy-start | bytes 2752516
  35.5 3.9 %collective-permute-start.7 = (bf16[16,32,896]{2,1,0:T(8,128)(2,1)S(1)}, bf16[16,32,896]{2,1,0:T(8,128)(2,1)S(1)}, u32[]{:S(2)}, u32[]{:S(2)}) collective-permute-start(bf16[16,32,896]{2,1,0:T(8,128)(2,1)S(1)} %constant_dynamic-update-slice_fusion.5.own_ref), channel_id=1, source_target_pairs={{0,16},{16,0},{1,17},{17,1},{2,18},{18,2},{3,19},{19,3},{4,20},{20... | collective-permute-start | bytes 2752520 | tf_op jit(solution)/shard_map/ppermute | solution.py:800
  39.4 1.9 copy-start.12
  39.5 11.3 %collective-permute-start.11 = (bf16[4,32,2304]{2,1,0:T(8,128)(2,1)S(1)}, bf16[4,32,2304]{2,1,0:T(8,128)(2,1)S(1)}, u32[]{:S(2)}, u32[]{:S(2)}) collective-permute-start(bf16[4,32,2304]{2,1,0:T(8,128)(2,1)S(1)} %pad_maximum_fusion), channel_id=1, source_target_pairs={{0,2},{1,3},{2,0},{3,1},{4,6},{5,7},{6,4},{7,5},{8,10},{9,11},{10,... | collective-permute-start | bytes 1769480 | tf_op jit(solution)/shard_map/ppermute | solution.py:922
  50.9 19.8 %collective-permute-start.12 = (bf16[8,32,2304]{2,1,0:T(8,128)(2,1)S(1)}, bf16[8,32,2304]{2,1,0:T(8,128)(2,1)S(1)}, u32[]{:S(2)}, u32[]{:S(2)}) collective-permute-start(bf16[8,32,2304]{2,1,0:T(8,128)(2,1)S(1)} %get-tuple-element.273), channel_id=1, source_target_pairs={{0,1},{1,0},{2,3},{3,2},{4,5},{5,4},{6,7},{7,6},{8,9},{9,8},{10,11... | collective-permute-start | bytes 3538952 | tf_op jit(solution)/shard_map/ppermute | solution.py:922
  70.8 13.4 %copy-start.8 = (bf16[16,32,2304]{2,1,0:T(8,128)(2,1)}, bf16[16,32,2304]{2,1,0:T(8,128)(2,1)S(1)}, u32[]{:S(2)}) copy-start(bf16[16,32,2304]{2,1,0:T(8,128)(2,1)S(1)} %constant_dynamic-update-slice_fusion.16.own_ref) | copy-start | bytes 7077892
  70.8 13.4 %collective-permute-start.13 = (bf16[16,32,2304]{2,1,0:T(8,128)(2,1)S(1)}, bf16[16,32,2304]{2,1,0:T(8,128)(2,1)S(1)}, u32[]{:S(2)}, u32[]{:S(2)}) collective-permute-start(bf16[16,32,2304]{2,1,0:T(8,128)(2,1)S(1)} %constant_dynamic-update-slice_fusion.16.own_ref), channel_id=1, source_target_pairs={{0,16},{16,0},{1,17},{17,1},{2,18},{18,2},{3,19},{19,3},{4,20},{20... | collective-permute-start | bytes 7077896 | tf_op jit(solution)/shard_map/ppermute | solution.py:800
  84.2 1.4 copy-start.10
  128.2 22.6 %collective-permute-start.14 = (bf16[16,32,2304]{2,1,0:T(8,128)(2,1)}, bf16[16,32,2304]{2,1,0:T(8,128)(2,1)S(1)}, u32[]{:S(2)}, u32[]{:S(2)}) collective-permute-start(bf16[16,32,2304]{2,1,0:T(8,128)(2,1)} %get-tuple-element.201), channel_id=1, source_target_pairs={{0,16},{16,0},{1,17},{17,1},{2,18},{18,2},{3,19},{19,3},{4,20},{20... | collective-permute-start | bytes 7077896 | tf_op jit(solution)/shard_map/ppermute | solution.py:800
  128.3 22.5 %copy-start.1 = (bf16[16,32,2304]{2,1,0:T(8,128)(2,1)S(1)}, bf16[16,32,2304]{2,1,0:T(8,128)(2,1)}, u32[]{:S(2)}) copy-start(bf16[16,32,2304]{2,1,0:T(8,128)(2,1)} %get-tuple-element.214) | copy-start | bytes 7077892
  151.4 0.9 copy-start.7
  151.5 23.2 %collective-permute-start.15 = (bf16[8,32,2304]{2,1,0:T(8,128)(2,1)S(1)}, bf16[8,32,2304]{2,1,0:T(8,128)(2,1)S(1)}, u32[]{:S(2)}, u32[]{:S(2)}) collective-permute-start(bf16[8,32,2304]{2,1,0:T(8,128)(2,1)S(1)} %slice.74), channel_id=1, source_target_pairs={{0,1},{1,0},{2,3},{3,2},{4,5},{5,4},{6,7},{7,6},{8,9},{9,8},{10,11... | collective-permute-start | bytes 3538952 | tf_op jit(solution)/shard_map/ppermute | solution.py:922
  174.7 1.1 copy-start.6
  175.1 17.1 %collective-permute-start.16 = (bf16[4,32,2304]{2,1,0:T(8,128)(2,1)S(1)}, bf16[4,32,2304]{2,1,0:T(8,128)(2,1)S(1)}, u32[]{:S(2)}, u32[]{:S(2)}) collective-permute-start(bf16[4,32,2304]{2,1,0:T(8,128)(2,1)S(1)} %slice.76), channel_id=1, source_target_pairs={{0,2},{1,3},{2,0},{3,1},{4,6},{5,7},{6,4},{7,5},{8,10},{9,11},{10,... | collective-permute-start | bytes 1769480 | tf_op jit(solution)/shard_map/ppermute | solution.py:922
  176.0 16.2 %collective-permute-start.17 = (bf16[16,2816]{1,0:T(8,128)(2,1)S(1)}, bf16[16,2816]{1,0:T(8,128)(2,1)S(1)}, u32[]{:S(2)}, u32[]{:S(2)}) collective-permute-start(bf16[16,2816]{1,0:T(8,128)(2,1)S(1)} %convert_element_type.151), channel_id=1, source_target_pairs={{0,16},{16,0},{1,17},{17,1},{2,18},{18,2},{3,19},{19,3},{4,20},{20... | collective-permute-start | bytes 270344 | tf_op jit(solution)/shard_map/ppermute | solution.py:989
  192.2 10.2 %collective-permute-start.18 = (bf16[16,32,896]{2,1,0:T(8,128)(2,1)}, bf16[16,32,896]{2,1,0:T(8,128)(2,1)S(1)}, u32[]{:S(2)}, u32[]{:S(2)}) collective-permute-start(bf16[16,32,896]{2,1,0:T(8,128)(2,1)} %get-tuple-element.229), channel_id=1, source_target_pairs={{0,16},{16,0},{1,17},{17,1},{2,18},{18,2},{3,19},{19,3},{4,20},{20... | collective-permute-start | bytes 2752520 | tf_op jit(solution)/shard_map/ppermute | solution.py:800
  192.5 9.8 %collective-permute-start.19 = (bf16[16,2816]{1,0:T(8,128)(2,1)S(1)}, bf16[16,2816]{1,0:T(8,128)(2,1)S(1)}, u32[]{:S(2)}, u32[]{:S(2)}) collective-permute-start(bf16[16,2816]{1,0:T(8,128)(2,1)S(1)} %add_convert_fusion.8), channel_id=1, source_target_pairs={{0,1},{1,0},{2,3},{3,2},{4,5},{5,4},{6,7},{7,6},{8,9},{9,8},{10,11... | collective-permute-start | bytes 270344 | tf_op jit(solution)/shard_map/ppermute | solution.py:989
  194.1 9.4 %collective-permute-start.22 = (bf16[32,2304]{1,0:T(8,128)(2,1)S(1)}, bf16[32,2304]{1,0:T(8,128)(2,1)S(1)}, u32[]{:S(2)}, u32[]{:S(2)}) collective-permute-start(bf16[32,2304]{1,0:T(8,128)(2,1)S(1)} %get-tuple-element.271), channel_id=1, source_target_pairs={{0,4},{1,5},{2,6},{3,7},{4,0},{5,1},{6,2},{7,3},{8,12},{9,13},{10,... | collective-permute-start | bytes 442376 | tf_op jit(solution)/shard_map/ppermute | solution.py:922
  194.6 14.8 %collective-permute-start.23 = (bf16[32,2304]{1,0:T(8,128)(2,1)S(1)}, bf16[32,2304]{1,0:T(8,128)(2,1)S(1)}, u32[]{:S(2)}, u32[]{:S(2)}) collective-permute-start(bf16[32,2304]{1,0:T(8,128)(2,1)S(1)} %get-tuple-element.270), channel_id=1, source_target_pairs={{0,8},{1,9},{2,10},{3,11},{4,12},{5,13},{6,14},{7,15},{8,0},{9,1},... | collective-permute-start | bytes 442376 | tf_op jit(solution)/shard_map/ppermute | solution.py:922
  198.3 4.0 %copy-start.3 = (bf16[16,32,896]{2,1,0:T(8,128)(2,1)S(1)}, bf16[16,32,896]{2,1,0:T(8,128)(2,1)}, u32[]{:S(2)}) copy-start(bf16[16,32,896]{2,1,0:T(8,128)(2,1)} %get-tuple-element.222) | copy-start | bytes 2752516
  198.3 11.0 %collective-permute-start.24 = (bf16[32,2304]{1,0:T(8,128)(2,1)S(1)}, bf16[32,2304]{1,0:T(8,128)(2,1)S(1)}, u32[]{:S(2)}, u32[]{:S(2)}) collective-permute-start(bf16[32,2304]{1,0:T(8,128)(2,1)S(1)} %get-tuple-element.269), channel_id=1, source_target_pairs={{0,12},{1,13},{2,14},{3,15},{4,8},{5,9},{6,10},{7,11},{8,4},{9,5},... | collective-permute-start | bytes 442376 | tf_op jit(solution)/shard_map/ppermute | solution.py:922
  202.3 1.2 copy-start.14
  202.6 8.5 %collective-permute-start.20 = (bf16[8,32,896]{2,1,0:T(8,128)(2,1)S(1)}, bf16[8,32,896]{2,1,0:T(8,128)(2,1)S(1)}, u32[]{:S(2)}, u32[]{:S(2)}) collective-permute-start(bf16[8,32,896]{2,1,0:T(8,128)(2,1)S(1)} %slice.78), channel_id=1, source_target_pairs={{0,1},{1,0},{2,3},{3,2},{4,5},{5,4},{6,7},{7,6},{8,9},{9,8},{10,11... | collective-permute-start | bytes 1376264 | tf_op jit(solution)/shard_map/ppermute | solution.py:922
  203.5 7.7 %collective-permute-start.25 = (bf16[4,208,512]{2,1,0:T(8,128)(2,1)S(1)}, bf16[4,208,512]{2,1,0:T(8,128)(2,1)S(1)}, u32[]{:S(2)}, u32[]{:S(2)}) collective-permute-start(bf16[4,208,512]{2,1,0:T(8,128)(2,1)S(1)} %copy-done.14), channel_id=1, source_target_pairs={{0,16},{16,0},{1,17},{17,1},{2,18},{18,2},{3,19},{19,3},{4,20},{20... | collective-permute-start | bytes 2555912 | tf_op jit(solution)/shard_map/ppermute | solution.py:800
  203.5 5.8 %collective-permute-start.21 = (bf16[16,2816]{1,0:T(8,128)(2,1)S(1)}, bf16[16,2816]{1,0:T(8,128)(2,1)S(1)}, u32[]{:S(2)}, u32[]{:S(2)}) collective-permute-start(bf16[16,2816]{1,0:T(8,128)(2,1)S(1)} %add_convert_fusion.7), channel_id=1, source_target_pairs={{0,2},{1,3},{2,0},{3,1},{4,6},{5,7},{6,4},{7,5},{8,10},{9,11},{10,... | collective-permute-start | bytes 270344 | tf_op jit(solution)/shard_map/ppermute | solution.py:989
  204.9 13.0 %copy-start = (f32[4,392,512]{2,1,0:T(8,128)S(1)}, f32[4,392,512]{2,1,0:T(8,128)}, u32[]{:S(2)}) copy-start(f32[4,392,512]{2,1,0:T(8,128)} %get-tuple-element.245) | copy-start | bytes 9633796
  208.5 8.7 %copy-start.13 = (bf16[4,208,512]{2,1,0:T(8,128)(2,1)S(1)}, bf16[4,208,512]{2,1,0:T(8,128)(2,1)}, u32[]{:S(2)}) copy-start(bf16[4,208,512]{2,1,0:T(8,128)(2,1)} %get-tuple-element.249) | copy-start | bytes 2555908
  211.2 6.1 %collective-permute-start.27 = (bf16[16,2816]{1,0:T(8,128)(2,1)S(1)}, bf16[16,2816]{1,0:T(8,128)(2,1)S(1)}, u32[]{:S(2)}, u32[]{:S(2)}) collective-permute-start(bf16[16,2816]{1,0:T(8,128)(2,1)S(1)} %add_convert_fusion.6), channel_id=1, source_target_pairs={{0,4},{1,5},{2,6},{3,7},{4,0},{5,1},{6,2},{7,3},{8,12},{9,13},{10,... | collective-permute-start | bytes 270344 | tf_op jit(solution)/shard_map/ppermute | solution.py:922
  212.2 10.4 %collective-permute-start.28 = (bf16[16,2816]{1,0:T(8,128)(2,1)S(1)}, bf16[16,2816]{1,0:T(8,128)(2,1)S(1)}, u32[]{:S(2)}, u32[]{:S(2)}) collective-permute-start(bf16[16,2816]{1,0:T(8,128)(2,1)S(1)} %add_convert_fusion.6), channel_id=1, source_target_pairs={{0,8},{1,9},{2,10},{3,11},{4,12},{5,13},{6,14},{7,15},{8,0},{9,1},... | collective-permute-start | bytes 270344 | tf_op jit(solution)/shard_map/ppermute | solution.py:922
  215.4 7.2 %collective-permute-start.29 = (bf16[16,2816]{1,0:T(8,128)(2,1)S(1)}, bf16[16,2816]{1,0:T(8,128)(2,1)S(1)}, u32[]{:S(2)}, u32[]{:S(2)}) collective-permute-start(bf16[16,2816]{1,0:T(8,128)(2,1)S(1)} %add_convert_fusion.6), channel_id=1, source_target_pairs={{0,12},{1,13},{2,14},{3,15},{4,8},{5,9},{6,10},{7,11},{8,4},{9,5},... | collective-permute-start | bytes 270344 | tf_op jit(solution)/shard_map/ppermute | solution.py:922
  215.8 6.8 %collective-permute-start.26 = (bf16[4,32,896]{2,1,0:T(8,128)(2,1)S(1)}, bf16[4,32,896]{2,1,0:T(8,128)(2,1)S(1)}, u32[]{:S(2)}, u32[]{:S(2)}) collective-permute-start(bf16[4,32,896]{2,1,0:T(8,128)(2,1)S(1)} %slice.84), channel_id=1, source_target_pairs={{0,2},{1,3},{2,0},{3,1},{4,6},{5,7},{6,4},{7,5},{8,10},{9,11},{10,... | collective-permute-start | bytes 688136 | tf_op jit(solution)/shard_map/ppermute | solution.py:922
  217.2 5.4 %collective-permute-start.31 = (bf16[4,208,512]{2,1,0:T(8,128)(2,1)S(1)}, bf16[4,208,512]{2,1,0:T(8,128)(2,1)S(1)}, u32[]{:S(2)}, u32[]{:S(2)}) collective-permute-start(bf16[4,208,512]{2,1,0:T(8,128)(2,1)S(1)} %copy-done.13), channel_id=1, source_target_pairs={{0,16},{16,0},{1,17},{17,1},{2,18},{18,2},{3,19},{19,3},{4,20},{20... | collective-permute-start | bytes 2555912 | tf_op jit(solution)/shard_map/ppermute | solution.py:800
  217.3 5.3 %collective-permute-start.30 = (bf16[32,2304]{1,0:T(8,128)(2,1)S(1)}, bf16[32,2304]{1,0:T(8,128)(2,1)S(1)}, u32[]{:S(2)}, u32[]{:S(2)}) collective-permute-start(bf16[32,2304]{1,0:T(8,128)(2,1)S(1)} %fusion.7), channel_id=1, source_target_pairs={{0,16},{16,0},{1,17},{17,1},{2,18},{18,2},{3,19},{19,3},{4,20},{20... | collective-permute-start | bytes 442376 | tf_op jit(solution)/shard_map/ppermute | solution.py:800
  219.9 7.5 %copy-start.2 = (bf16[4,392,512]{2,1,0:T(8,128)(2,1)S(1)}, bf16[4,392,512]{2,1,0:T(8,128)(2,1)}, u32[]{:S(2)}) copy-start(bf16[4,392,512]{2,1,0:T(8,128)(2,1)} %get-tuple-element.252) | copy-start | bytes 4816900
  222.9 14.3 %collective-permute-start.32 = (bf16[32,896]{1,0:T(8,128)(2,1)S(1)}, bf16[32,896]{1,0:T(8,128)(2,1)S(1)}, u32[]{:S(2)}, u32[]{:S(2)}) collective-permute-start(bf16[32,896]{1,0:T(8,128)(2,1)S(1)} %get-tuple-element.280), channel_id=1, source_target_pairs={{0,4},{1,5},{2,6},{3,7},{4,0},{5,1},{6,2},{7,3},{8,12},{9,13},{10,... | collective-permute-start | bytes 172040 | tf_op jit(solution)/shard_map/ppermute | solution.py:922
  224.7 12.5 %collective-permute-start.33 = (bf16[32,896]{1,0:T(8,128)(2,1)S(1)}, bf16[32,896]{1,0:T(8,128)(2,1)S(1)}, u32[]{:S(2)}, u32[]{:S(2)}) collective-permute-start(bf16[32,896]{1,0:T(8,128)(2,1)S(1)} %get-tuple-element.279), channel_id=1, source_target_pairs={{0,8},{1,9},{2,10},{3,11},{4,12},{5,13},{6,14},{7,15},{8,0},{9,1},... | collective-permute-start | bytes 172040 | tf_op jit(solution)/shard_map/ppermute | solution.py:922
  226.4 10.9 %collective-permute-start.34 = (bf16[32,896]{1,0:T(8,128)(2,1)S(1)}, bf16[32,896]{1,0:T(8,128)(2,1)S(1)}, u32[]{:S(2)}, u32[]{:S(2)}) collective-permute-start(bf16[32,896]{1,0:T(8,128)(2,1)S(1)} %get-tuple-element.278), channel_id=1, source_target_pairs={{0,12},{1,13},{2,14},{3,15},{4,8},{5,9},{6,10},{7,11},{8,4},{9,5},... | collective-permute-start | bytes 172040 | tf_op jit(solution)/shard_map/ppermute | solution.py:922
  237.9 1.2 collective-permute-start.35

commit v2 on v1

--- a/solution.py
+++ b/solution.py
@@ -73,6 +73,8 @@
     totals.append(context(PAIR - 1))
     every = jnp.concatenate(totals, axis=0)
     ordinary = jnp.logical_and(jnp.min(every) > 1.0 / SAFE, jnp.max(every) < SAFE)
+
+    ctx_tok_ref[0] = jnp.transpose(ctx_ref[0])
 
     @pl.when(jnp.logical_not(ordinary))
     def _():
@@ -94,8 +96,7 @@
             return carry
 
         lax.fori_loop(0, PAIR, again, 0)
-
-    ctx_tok_ref[0] = jnp.transpose(ctx_ref[0])
+        ctx_tok_ref[0] = jnp.transpose(ctx_ref[0])
 
 
 def attend(side,qT,k,vT,bias,mq,mk):

time: 245 us -> 244 us (level)
  no operation moved by 1% of the time
where the time goes in v2:
time: 244 us; the launch traced here: 239 us
  Pallas kernels  178 us (73%)
  starting transfers between devices  38.1 us (16%)
  other arithmetic  8.99 us (4%)
  waiting for transfers between devices  7.15 us (3%)
  local copies, waits for them, and re-layouts  5.41 us (2%)
    pallas_call x2, Pallas kernels, attend_back(): pl.pallas_call(back_kernel, grid=(2, nw), in_specs=[pl.BlockSpec((1, GROU...  44.9 us
    pallas_call x1, Pallas kernels, feed(): pl.pallas_call(feed_kernel, grid_spec=pltpu.PrefetchScalarGridSpec(num_sc...  42.6 us
    ppermute x23, starting transfers between devices, hop(): return lax.ppermute(part, ('seq', 'shard'), pairs)  33.3 us
    pallas_call x2, Pallas kernels, attend(): pl.pallas_call(attend_kernel, grid=(nw,), in_specs=[pl.BlockSpec((1, half...  25.1 us
    pallas_call x1, Pallas kernels, input_side(): pl.pallas_call(input_kernel, grid_spec=pltpu.PrefetchScalarGridSpec(num_s...  15.9 us
    pallas_call x2, Pallas kernels, bias_half(): pl.pallas_call(bias_kernel, grid=(1,), in_specs=[pl.BlockSpec((8 * heads,...  11.5 us
    pallas_call x1, Pallas kernels, project(): pl.pallas_call(project_kernel, grid_spec=pltpu.PrefetchScalarGridSpec(num...  9.49 us
    pallas_call x2, Pallas kernels, enter(): pl.pallas_call(enter_kernel, grid=(2,), in_specs=[part, part, pl.BlockSpe...  7.67 us
  transfers between devices with their start and end apart: 36, of which 6 were waited for; matrix products, arithmetic and copies ran while one was open for 4% of the time, Pallas kernels for 57%

profile of v2, /device:TPU:0, one launch (start us, length us, event | category | flops | bytes accessed | tf_op | source)
XLA Modules:
  0.0 239.5 jit_solution(7065854105085915560)
XLA Ops:
  0.7 0.5 collective-permute-start.3
  1.2 1.9 pack.1
  3.0 2.6 %collective-permute-start = (bf16[32,896]{1,0:T(8,128)(2,1)}, bf16[32,896]{1,0:T(8,128)(2,1)S(1)}, u32[]{:S(2)}, u32[]{:S(2)}) collective-permute-start(bf16[32,896]{1,0:T(8,128)(2,1)} %get-tuple-element.141), channel_id=1, source_target_pairs={{0,4},{1,5},{2,6},{3,7},{4,0},{5,1},{6,2},{7,3},{8,12},{9,13},{10,... | collective-permute-start | bytes 172040 | tf_op jit(solution)/shard_map/ppermute | solution.py:923
  5.6 2.6 %collective-permute-start.1 = (bf16[32,896]{1,0:T(8,128)(2,1)}, bf16[32,896]{1,0:T(8,128)(2,1)S(1)}, u32[]{:S(2)}, u32[]{:S(2)}) collective-permute-start(bf16[32,896]{1,0:T(8,128)(2,1)} %get-tuple-element.141), channel_id=1, source_target_pairs={{0,8},{1,9},{2,10},{3,11},{4,12},{5,13},{6,14},{7,15},{8,0},{9,1},... | collective-permute-start | bytes 172040 | tf_op jit(solution)/shard_map/ppermute | solution.py:923
  8.2 0.9 collective-permute-start.8
  9.1 0.8 constant_dynamic-update-slice_fusion.4
  10.0 6.4 %prepare.1 = (s32[2,2816]{1,0:T(2,128)}, f32[128,1408]{1,0:T(8,128)}, bf16[4,392,128]{2,1,0:T(8,128)(2,1)}, bf16[4,32,392]{2,1,0:T(8,128)(2,1)}) custom-call(s32[392,392]{1,0:T(8,128)} %rel_ref.1, s32[4,2816]{1,0:T(4,128)} %constant.116.clone.maps_ref, bf16[16,2535]{1,0:T(8,128)(2,1)} %bitcast.85, s32[4,392]{1,0:T(4,128)} %region_ref.1, ...), custom_call_target="tpu_custom_call" | custom-call | flops 6000000000 | bytes 21600000 | tf_op jit(solution)/shard_map/prepare/pallas_call | solution.py:313
  16.4 0.6 concatenate.35.places_ref
  17.1 3.5 %collective-permute-start.9 = (bf16[32,2304]{1,0:T(8,128)(2,1)S(1)}, bf16[32,2304]{1,0:T(8,128)(2,1)S(1)}, u32[]{:S(2)}, u32[]{:S(2)}) collective-permute-start(bf16[32,2304]{1,0:T(8,128)(2,1)S(1)} %copy-done.4), channel_id=1, source_target_pairs={{0,8},{1,9},{2,10},{3,11},{4,12},{5,13},{6,14},{7,15},{8,0},{9,1},... | collective-permute-start | bytes 442376 | tf_op jit(solution)/shard_map/ppermute | solution.py:923
  20.7 1.7 collective-permute-start.4
  22.4 3.9 %enter.2.x_ref = bf16[4,392,512]{2,1,0:T(8,128)(2,1)} custom-call(bf16[4,392,512]{2,1,0:T(8,128)(2,1)} %bitcast.81, bf16[4,392,512]{2,1,0:T(8,128)(2,1)} %bitcast.9.arrived_ref, bf16[392,392]{1,0:T(8,128)(2,1)} %constant.111.clone.order_ref), custom_call_target="tpu_custom_call" | custom-call | flops 4000000000 | bytes 14400000 | tf_op jit(solution)/shard_map/enter/pallas_call | solution.py:837
  26.4 0.4 collective-permute-done.4
  26.8 1.7 collective-permute-start.5
  28.5 5.8 %position_bias.2.bias_ref = bf16[8,392,392]{2,1,0:T(8,128)(2,1)} custom-call(f32[128,1408]{1,0:T(8,128)} %get-tuple-element.178.narrow_ref, s32[392,128]{1,0:T(8,128)} %constant.113.clone.spot_ref), custom_call_target="tpu_custom_call" | custom-call | flops 5000000000 | bytes 18000000 | tf_op jit(solution)/shard_map/position_bias/pallas_call | solution.py:355
  34.3 1.1 collective-permute-done.5
  35.6 3.8 %enter.3.og_ref = bf16[4,392,512]{2,1,0:T(8,128)(2,1)} custom-call(bf16[4,392,512]{2,1,0:T(8,128)(2,1)} %bitcast.82, bf16[4,392,512]{2,1,0:T(8,128)(2,1)} %bitcast.83, bf16[392,392]{1,0:T(8,128)(2,1)} %constant.111.clone.order_ref), custom_call_target="tpu_custom_call" | custom-call | flops 4000000000 | bytes 14400000 | tf_op jit(solution)/shard_map/enter/pallas_call | solution.py:837
  39.5 1.7 collective-permute-start.11
  41.3 9.5 %project.1 = (bf16[4,512,392]{2,1,0:T(8,128)(2,1)}, bf16[4,512,392]{2,1,0:T(8,128)(2,1)}, bf16[4,512,392]{2,1,0:T(8,128)(2,1)}, bf16[4,392,512]{2,1,0:T(8,128)(2...) custom-call(s32[65]{0:T(128)} %concatenate.35.places_ref, bf16[4,392,512]{2,1,0:T(8,128)(2,1)} %enter.2.x_ref, ...), custom_call_target="tpu_custom_call" | custom-call | flops 8999999488 | bytes 32400000 | tf_op jit(solution)/shard_map/project/pallas_call | solution.py:469
  50.9 1.6 collective-permute-start.12
  52.5 12.1 %attend.2 = (bf16[4,256,392]{2,1,0:T(8,128)(2,1)}, bf16[4,392,256]{2,1,0:T(8,128)(2,1)}, bf16[4,8,392,392]{3,2,1,0:T(8,128)(2,1)}, f32[4,8,392]{2,1,0:T(8,128)}) custom-call(bf16[4,512,392]{2,1,0:T(8,128)(2,1)} %get-tuple-element.182.q_ref, bf16[4,392,512]{2,1,0:T(8,128)(2,1)} %get-tuple-element.164.k_ref, bf16[4,512,392]{2,1,0:T(8,128)(2,1)} %get-tuple-element.165.v_ref, ...), custom_call_target="tpu_custom_call" | custom-call | flops 10000000000 | bytes 36000000 | tf_op jit(solution)/shard_map/attend/pallas_call | solution.py:106
  64.6 5.8 %position_bias.3.bias_ref = bf16[8,392,392]{2,1,0:T(8,128)(2,1)} custom-call(f32[128,1408]{1,0:T(8,128)} %get-tuple-element.178.narrow_ref, s32[392,128]{1,0:T(8,128)} %constant.113.clone.spot_ref), custom_call_target="tpu_custom_call" | custom-call | flops 5000000000 | bytes 18000000 | tf_op jit(solution)/shard_map/position_bias/pallas_call | solution.py:355
  70.6 13.0 %attend.3 = (bf16[4,256,392]{2,1,0:T(8,128)(2,1)}, bf16[4,392,256]{2,1,0:T(8,128)(2,1)}, bf16[4,8,392,392]{3,2,1,0:T(8,128)(2,1)}, f32[4,8,392]{2,1,0:T(8,128)}) custom-call(bf16[4,512,392]{2,1,0:T(8,128)(2,1)} %get-tuple-element.182.q_ref, bf16[4,392,512]{2,1,0:T(8,128)(2,1)} %get-tuple-element.164.k_ref, bf16[4,512,392]{2,1,0:T(8,128)(2,1)} %get-tuple-element.165.v_ref, ...), custom_call_target="tpu_custom_call" | custom-call | flops 10000000000 | bytes 36000000 | tf_op jit(solution)/shard_map/attend/pallas_call | solution.py:106
  83.6 1.4 copy-done.10
  85.0 42.6 %feed_forward.1 = (bf16[4,392,512]{2,1,0:T(8,128)(2,1)}, f32[4,392,512]{2,1,0:T(8,128)}, bf16[4,512,392]{2,1,0:T(8,128)(2,1)}, bf16[16,32,2304]{2,1,0:T(8,128)(2...) custom-call(s32[65]{0:T(128)} %concatenate.35.places_ref, bf16[4,392,512]{2,1,0:T(8,128)(2,1)} %enter.2.x_ref, ...), custom_call_target="tpu_custom_call" | custom-call | flops 44000002048 | bytes 158400000 | tf_op jit(solution)/shard_map/feed_forward/pallas_call | solution.py:597
  127.7 22.5 %attend_back.2 = (bf16[4,392,256]{2,1,0:T(8,128)(2,1)}, bf16[4,392,256]{2,1,0:T(8,128)(2,1)}, bf16[4,392,256]{2,1,0:T(8,128)(2,1)}, f32[2,4,2816]{2,1,0:T(4,128)}) custom-call(bf16[4,8,392,392]{3,2,1,0:T(8,128)(2,1)} %get-tuple-element.179.e_ref, bf16[4,512,392]{2,1,0:T(8,128)(2,1)} %get-tuple-element.180.k_ref, ...), custom_call_target="tpu_custom_call" | custom-call | flops 20000000000 | bytes 72000000 | tf_op jit(solution)/shard_map/attend_back/pallas_call | solution.py:235
  150.2 0.6 add_convert_fusion
  150.9 0.7 collective-permute-start.15
  151.7 22.4 %attend_back.3 = (bf16[4,392,256]{2,1,0:T(8,128)(2,1)}, bf16[4,392,256]{2,1,0:T(8,128)(2,1)}, bf16[4,392,256]{2,1,0:T(8,128)(2,1)}, f32[2,4,2816]{2,1,0:T(4,128)}) custom-call(bf16[4,8,392,392]{3,2,1,0:T(8,128)(2,1)} %get-tuple-element.206.e_ref, bf16[4,512,392]{2,1,0:T(8,128)(2,1)} %get-tuple-element.180.k_ref, ...), custom_call_target="tpu_custom_call" | custom-call | flops 20000000000 | bytes 72000000 | tf_op jit(solution)/shard_map/attend_back/pallas_call | solution.py:235
  174.1 0.3 add_convert_fusion.1
  174.4 0.8 collective-permute-start.16
  175.3 0.3 collective-permute-start.17
  175.6 15.9 %input_side.1 = (bf16[4,392,512]{2,1,0:T(8,128)(2,1)}, bf16[16,32,896]{2,1,0:T(8,128)(2,1)}, bf16[16,32,896]{2,1,0:T(8,128)(2,1)}) custom-call(s32[65]{0:T(128)} %concatenate.35.places_ref, bf16[4,392,512]{2,1,0:T(8,128)(2,1)} %enter.2.x_ref, bf16[4,392,256]{2,1,0:T(8,128)(2,1)} %get-tuple-element.203.dq0, bf16[4,392,256]{2,1,0:T(8,128)(2,1)} %get-tuple-element.204.dk0, ...), custom_call_target="tpu_custom_call" | custom-call | flops 15000000512 | bytes 54000000 | tf_op jit(solution)/shard_map/input_side/pallas_call | solution.py:691
  191.6 0.3 collective-permute-start.18
  191.9 1.4 collective-permute-start.19
  193.5 0.5 collective-permute-start.22
  194.0 3.7 %collective-permute-start.23 = (bf16[32,2304]{1,0:T(8,128)(2,1)S(1)}, bf16[32,2304]{1,0:T(8,128)(2,1)S(1)}, u32[]{:S(2)}, u32[]{:S(2)}) collective-permute-start(bf16[32,2304]{1,0:T(8,128)(2,1)S(1)} %get-tuple-element.270), channel_id=1, source_target_pairs={{0,8},{1,9},{2,10},{3,11},{4,12},{5,13},{6,14},{7,15},{8,0},{9,1},... | collective-permute-start | bytes 442376 | tf_op jit(solution)/shard_map/ppermute | solution.py:923
  197.7 0.2 collective-permute-start.24
  197.9 3.8 %leave.2 = (f32[4,392,512]{2,1,0:T(8,128)}, bf16[4,208,512]{2,1,0:T(8,128)(2,1)}) custom-call(bf16[4,392,512]{2,1,0:T(8,128)(2,1)} %get-tuple-element.231.rows_ref, bf16[392,392]{1,0:T(8,128)(2,1)} %constant.124.order_ref), custom_call_target="tpu_custom_call" | custom-call | flops 4000000000 | bytes 14400000 | tf_op jit(solution)/shard_map/leave/pallas_call | solution.py:856
  201.8 0.2 add_convert_fusion.2
  202.0 0.8 collective-permute-start.20
  202.9 1.4 collective-permute-start.21
  204.3 3.6 %leave.3 = (bf16[4,392,512]{2,1,0:T(8,128)(2,1)}, bf16[4,208,512]{2,1,0:T(8,128)(2,1)}) custom-call(bf16[4,392,512]{2,1,0:T(8,128)(2,1)} %get-tuple-element.239.rows_ref, bf16[392,392]{1,0:T(8,128)(2,1)} %constant.124.order_ref), custom_call_target="tpu_custom_call" | custom-call | flops 4000000000 | bytes 14400000 | tf_op jit(solution)/shard_map/leave/pallas_call | solution.py:856
  207.9 0.9 collective-permute-done.23
  208.7 1.8 collective-permute-done.20
  210.6 1.0 collective-permute-start.27
  211.6 3.2 %collective-permute-start.28 = (bf16[16,2816]{1,0:T(8,128)(2,1)S(1)}, bf16[16,2816]{1,0:T(8,128)(2,1)S(1)}, u32[]{:S(2)}, u32[]{:S(2)}) collective-permute-start(bf16[16,2816]{1,0:T(8,128)(2,1)S(1)} %add_convert_fusion.6), channel_id=1, source_target_pairs={{0,8},{1,9},{2,10},{3,11},{4,12},{5,13},{6,14},{7,15},{8,0},{9,1},... | collective-permute-start | bytes 270344 | tf_op jit(solution)/shard_map/ppermute | solution.py:923
  214.8 0.3 collective-permute-start.29
  215.2 1.4 collective-permute-start.26
  216.7 0.6 collective-permute-start.30
  217.3 2.0 select_bitcast_fusion
  219.3 2.7 %collective-permute-done.28 = bf16[16,2816]{1,0:T(8,128)(2,1)S(1)} collective-permute-done((bf16[16,2816]{1,0:T(8,128)(2,1)S(1)}, bf16[16,2816]{1,0:T(8,128)(2,1)S(1)}, u32[]{:S(2)}, u32[]{:S(2)}) %collective-permute-start.28) | collective-permute-done | bytes 90144 | tf_op jit(solution)/shard_map/ppermute | solution.py:923
  222.3 1.8 collective-permute-start.32
  224.1 1.6 collective-permute-start.33
  225.7 1.0 collective-permute-start.34
  226.8 1.6 select_bitcast_fusion.1
  228.3 0.7 pad_maximum_fusion.1
  229.0 0.7 pad_maximum_fusion.2
  229.7 0.7 add_add_fusion.g_ref
  230.5 5.5 %table_rows.1 = f32[16,2535]{1,0:T(8,128)} custom-call(s32[2,2816]{1,0:T(2,128)} %get-tuple-element.254.lab_ref, f32[16,2816]{1,0:T(8,128)} %add_add_fusion.g_ref), custom_call_target="tpu_custom_call" | custom-call | flops 5000000000 | bytes 18000000 | tf_op jit(solution)/shard_map/table_rows/pallas_call | solution.py:381
  236.0 0.6 pad_maximum_fusion.6
  236.7 0.6 fusion.10
  237.3 0.5 slice_bitcast_fusion.9
  237.8 0.6 split.52
  238.6 0.7 pad_maximum_fusion.4
  (111 shorter events, 2.3 us)
Async XLA Ops:
  0.7 20.0 %collective-permute-start.3 = (bf16[1,4,392,512]{3,2,1,0:T(8,128)(2,1)}, bf16[1,4,392,512]{3,2,1,0:T(8,128)(2,1)}, u32[]{:S(2)}, u32[]{:S(2)}) collective-permute-start(bf16[1,4,392,512]{3,2,1,0:T(8,128)(2,1)} %param.24), channel_id=1, source_target_pairs={{0,16},{16,0},{1,17},{17,1},{2,18},{18,2},{3,19},{19,3},{4,20},{20... | collective-permute-start | bytes 4816904 | tf_op jit(solution)/shard_map/ppermute | solution.py:801
  3.0 14.0 %collective-permute-start = (bf16[32,896]{1,0:T(8,128)(2,1)}, bf16[32,896]{1,0:T(8,128)(2,1)S(1)}, u32[]{:S(2)}, u32[]{:S(2)}) collective-permute-start(bf16[32,896]{1,0:T(8,128)(2,1)} %get-tuple-element.141), channel_id=1, source_target_pairs={{0,4},{1,5},{2,6},{3,7},{4,0},{5,1},{6,2},{7,3},{8,12},{9,13},{10,... | collective-permute-start | bytes 172040 | tf_op jit(solution)/shard_map/ppermute | solution.py:923
  5.6 14.9 %collective-permute-start.1 = (bf16[32,896]{1,0:T(8,128)(2,1)}, bf16[32,896]{1,0:T(8,128)(2,1)S(1)}, u32[]{:S(2)}, u32[]{:S(2)}) collective-permute-start(bf16[32,896]{1,0:T(8,128)(2,1)} %get-tuple-element.141), channel_id=1, source_target_pairs={{0,8},{1,9},{2,10},{3,11},{4,12},{5,13},{6,14},{7,15},{8,0},{9,1},... | collective-permute-start | bytes 172040 | tf_op jit(solution)/shard_map/ppermute | solution.py:923
  8.2 12.3 %collective-permute-start.2 = (bf16[32,896]{1,0:T(8,128)(2,1)}, bf16[32,896]{1,0:T(8,128)(2,1)S(1)}, u32[]{:S(2)}, u32[]{:S(2)}) collective-permute-start(bf16[32,896]{1,0:T(8,128)(2,1)} %get-tuple-element.141), channel_id=1, source_target_pairs={{0,12},{1,13},{2,14},{3,15},{4,8},{5,9},{6,10},{7,11},{8,4},{9,5},... | collective-permute-start | bytes 172040 | tf_op jit(solution)/shard_map/ppermute | solution.py:923
  8.2 31.2 %collective-permute-start.8 = (bf16[32,2304]{1,0:T(8,128)(2,1)}, bf16[32,2304]{1,0:T(8,128)(2,1)S(1)}, u32[]{:S(2)}, u32[]{:S(2)}) collective-permute-start(bf16[32,2304]{1,0:T(8,128)(2,1)} %get-tuple-element.151), channel_id=1, source_target_pairs={{0,4},{1,5},{2,6},{3,7},{4,0},{5,1},{6,2},{7,3},{8,12},{9,13},{10,... | collective-permute-start | bytes 442376 | tf_op jit(solution)/shard_map/ppermute | solution.py:923
  10.0 7.1 %copy-start.4 = (bf16[32,2304]{1,0:T(8,128)(2,1)S(1)}, bf16[32,2304]{1,0:T(8,128)(2,1)}, u32[]{:S(2)}) copy-start(bf16[32,2304]{1,0:T(8,128)(2,1)} %get-tuple-element.151) | copy-start | bytes 442372
  10.0 10.7 %copy-start.5 = (bf16[32,896]{1,0:T(8,128)(2,1)S(1)}, bf16[32,896]{1,0:T(8,128)(2,1)}, u32[]{:S(2)}) copy-start(bf16[32,896]{1,0:T(8,128)(2,1)} %get-tuple-element.141) | copy-start | bytes 172036
  17.1 22.3 %collective-permute-start.9 = (bf16[32,2304]{1,0:T(8,128)(2,1)S(1)}, bf16[32,2304]{1,0:T(8,128)(2,1)S(1)}, u32[]{:S(2)}, u32[]{:S(2)}) collective-permute-start(bf16[32,2304]{1,0:T(8,128)(2,1)S(1)} %copy-done.4), channel_id=1, source_target_pairs={{0,8},{1,9},{2,10},{3,11},{4,12},{5,13},{6,14},{7,15},{8,0},{9,1},... | collective-permute-start | bytes 442376 | tf_op jit(solution)/shard_map/ppermute | solution.py:923
  20.5 18.8 %collective-permute-start.10 = (bf16[32,2304]{1,0:T(8,128)(2,1)S(1)}, bf16[32,2304]{1,0:T(8,128)(2,1)S(1)}, u32[]{:S(2)}, u32[]{:S(2)}) collective-permute-start(bf16[32,2304]{1,0:T(8,128)(2,1)S(1)} %copy-done.4), channel_id=1, source_target_pairs={{0,12},{1,13},{2,14},{3,15},{4,8},{5,9},{6,10},{7,11},{8,4},{9,5},... | collective-permute-start | bytes 442376 | tf_op jit(solution)/shard_map/ppermute | solution.py:923
  20.6 13.8 %collective-permute-start.6 = (bf16[1,4,392,512]{3,2,1,0:T(8,128)(2,1)}, bf16[1,4,392,512]{3,2,1,0:T(8,128)(2,1)S(1)}, u32[]{:S(2)}, u32[]{:S(2)}) collective-permute-start(bf16[1,4,392,512]{3,2,1,0:T(8,128)(2,1)} %param.40), channel_id=1, source_target_pairs={{0,16},{16,0},{1,17},{17,1},{2,18},{18,2},{3,19},{19,3},{4,20},{20... | collective-permute-start | bytes 4816904 | tf_op jit(solution)/shard_map/ppermute | solution.py:801
  20.7 6.1 %collective-permute-start.4 = (bf16[4,32,896]{2,1,0:T(8,128)(2,1)S(1)}, bf16[4,32,896]{2,1,0:T(8,128)(2,1)S(1)}, u32[]{:S(2)}, u32[]{:S(2)}) collective-permute-start(bf16[4,32,896]{2,1,0:T(8,128)(2,1)S(1)} %pad_maximum_fusion.3), channel_id=1, source_target_pairs={{0,2},{1,3},{2,0},{3,1},{4,6},{5,7},{6,4},{7,5},{8,10},{9,11},{10,... | collective-permute-start | bytes 688136 | tf_op jit(solution)/shard_map/ppermute | solution.py:923
  26.8 8.5 %collective-permute-start.5 = (bf16[8,32,896]{2,1,0:T(8,128)(2,1)S(1)}, bf16[8,32,896]{2,1,0:T(8,128)(2,1)S(1)}, u32[]{:S(2)}, u32[]{:S(2)}) collective-permute-start(bf16[8,32,896]{2,1,0:T(8,128)(2,1)S(1)} %get-tuple-element.281), channel_id=1, source_target_pairs={{0,1},{1,0},{2,3},{3,2},{4,5},{5,4},{6,7},{7,6},{8,9},{9,8},{10,11... | collective-permute-start | bytes 1376264 | tf_op jit(solution)/shard_map/ppermute | solution.py:923
  34.3 1.3 copy-start.11
  35.4 3.9 %copy-start.9 = (bf16[16,32,896]{2,1,0:T(8,128)(2,1)}, bf16[16,32,896]{2,1,0:T(8,128)(2,1)S(1)}, u32[]{:S(2)}) copy-start(bf16[16,32,896]{2,1,0:T(8,128)(2,1)S(1)} %constant_dynamic-update-slice_fusion.5.own_ref) | copy-start | bytes 2752516
  35.5 3.9 %collective-permute-start.7 = (bf16[16,32,896]{2,1,0:T(8,128)(2,1)S(1)}, bf16[16,32,896]{2,1,0:T(8,128)(2,1)S(1)}, u32[]{:S(2)}, u32[]{:S(2)}) collective-permute-start(bf16[16,32,896]{2,1,0:T(8,128)(2,1)S(1)} %constant_dynamic-update-slice_fusion.5.own_ref), channel_id=1, source_target_pairs={{0,16},{16,0},{1,17},{17,1},{2,18},{18,2},{3,19},{19,3},{4,20},{20... | collective-permute-start | bytes 2752520 | tf_op jit(solution)/shard_map/ppermute | solution.py:801
  39.4 1.9 copy-start.12
  39.5 11.3 %collective-permute-start.11 = (bf16[4,32,2304]{2,1,0:T(8,128)(2,1)S(1)}, bf16[4,32,2304]{2,1,0:T(8,128)(2,1)S(1)}, u32[]{:S(2)}, u32[]{:S(2)}) collective-permute-start(bf16[4,32,2304]{2,1,0:T(8,128)(2,1)S(1)} %pad_maximum_fusion), channel_id=1, source_target_pairs={{0,2},{1,3},{2,0},{3,1},{4,6},{5,7},{6,4},{7,5},{8,10},{9,11},{10,... | collective-permute-start | bytes 1769480 | tf_op jit(solution)/shard_map/ppermute | solution.py:923
  50.9 19.5 %collective-permute-start.12 = (bf16[8,32,2304]{2,1,0:T(8,128)(2,1)S(1)}, bf16[8,32,2304]{2,1,0:T(8,128)(2,1)S(1)}, u32[]{:S(2)}, u32[]{:S(2)}) collective-permute-start(bf16[8,32,2304]{2,1,0:T(8,128)(2,1)S(1)} %get-tuple-element.273), channel_id=1, source_target_pairs={{0,1},{1,0},{2,3},{3,2},{4,5},{5,4},{6,7},{7,6},{8,9},{9,8},{10,11... | collective-permute-start | bytes 3538952 | tf_op jit(solution)/shard_map/ppermute | solution.py:923
  70.5 13.1 %copy-start.8 = (bf16[16,32,2304]{2,1,0:T(8,128)(2,1)}, bf16[16,32,2304]{2,1,0:T(8,128)(2,1)S(1)}, u32[]{:S(2)}) copy-start(bf16[16,32,2304]{2,1,0:T(8,128)(2,1)S(1)} %constant_dynamic-update-slice_fusion.16.own_ref) | copy-start | bytes 7077892
  70.5 13.1 %collective-permute-start.13 = (bf16[16,32,2304]{2,1,0:T(8,128)(2,1)S(1)}, bf16[16,32,2304]{2,1,0:T(8,128)(2,1)S(1)}, u32[]{:S(2)}, u32[]{:S(2)}) collective-permute-start(bf16[16,32,2304]{2,1,0:T(8,128)(2,1)S(1)} %constant_dynamic-update-slice_fusion.16.own_ref), channel_id=1, source_target_pairs={{0,16},{16,0},{1,17},{17,1},{2,18},{18,2},{3,19},{19,3},{4,20},{20... | collective-permute-start | bytes 7077896 | tf_op jit(solution)/shard_map/ppermute | solution.py:801
  83.5 1.4 copy-start.10
  127.6 22.6 %collective-permute-start.14 = (bf16[16,32,2304]{2,1,0:T(8,128)(2,1)}, bf16[16,32,2304]{2,1,0:T(8,128)(2,1)S(1)}, u32[]{:S(2)}, u32[]{:S(2)}) collective-permute-start(bf16[16,32,2304]{2,1,0:T(8,128)(2,1)} %get-tuple-element.201), channel_id=1, source_target_pairs={{0,16},{16,0},{1,17},{17,1},{2,18},{18,2},{3,19},{19,3},{4,20},{20... | collective-permute-start | bytes 7077896 | tf_op jit(solution)/shard_map/ppermute | solution.py:801
  127.7 22.5 %copy-start.1 = (bf16[16,32,2304]{2,1,0:T(8,128)(2,1)S(1)}, bf16[16,32,2304]{2,1,0:T(8,128)(2,1)}, u32[]{:S(2)}) copy-start(bf16[16,32,2304]{2,1,0:T(8,128)(2,1)} %get-tuple-element.214) | copy-start | bytes 7077892
  150.8 0.9 copy-start.7
  150.9 23.2 %collective-permute-start.15 = (bf16[8,32,2304]{2,1,0:T(8,128)(2,1)S(1)}, bf16[8,32,2304]{2,1,0:T(8,128)(2,1)S(1)}, u32[]{:S(2)}, u32[]{:S(2)}) collective-permute-start(bf16[8,32,2304]{2,1,0:T(8,128)(2,1)S(1)} %slice.74), channel_id=1, source_target_pairs={{0,1},{1,0},{2,3},{3,2},{4,5},{5,4},{6,7},{7,6},{8,9},{9,8},{10,11... | collective-permute-start | bytes 3538952 | tf_op jit(solution)/shard_map/ppermute | solution.py:923
  174.1 1.1 copy-start.6
  174.4 17.1 %collective-permute-start.16 = (bf16[4,32,2304]{2,1,0:T(8,128)(2,1)S(1)}, bf16[4,32,2304]{2,1,0:T(8,128)(2,1)S(1)}, u32[]{:S(2)}, u32[]{:S(2)}) collective-permute-start(bf16[4,32,2304]{2,1,0:T(8,128)(2,1)S(1)} %slice.76), channel_id=1, source_target_pairs={{0,2},{1,3},{2,0},{3,1},{4,6},{5,7},{6,4},{7,5},{8,10},{9,11},{10,... | collective-permute-start | bytes 1769480 | tf_op jit(solution)/shard_map/ppermute | solution.py:923
  175.3 16.2 %collective-permute-start.17 = (bf16[16,2816]{1,0:T(8,128)(2,1)S(1)}, bf16[16,2816]{1,0:T(8,128)(2,1)S(1)}, u32[]{:S(2)}, u32[]{:S(2)}) collective-permute-start(bf16[16,2816]{1,0:T(8,128)(2,1)S(1)} %convert_element_type.151), channel_id=1, source_target_pairs={{0,16},{16,0},{1,17},{17,1},{2,18},{18,2},{3,19},{19,3},{4,20},{20... | collective-permute-start | bytes 270344 | tf_op jit(solution)/shard_map/ppermute | solution.py:990
  191.6 10.2 %collective-permute-start.18 = (bf16[16,32,896]{2,1,0:T(8,128)(2,1)}, bf16[16,32,896]{2,1,0:T(8,128)(2,1)S(1)}, u32[]{:S(2)}, u32[]{:S(2)}) collective-permute-start(bf16[16,32,896]{2,1,0:T(8,128)(2,1)} %get-tuple-element.229), channel_id=1, source_target_pairs={{0,16},{16,0},{1,17},{17,1},{2,18},{18,2},{3,19},{19,3},{4,20},{20... | collective-permute-start | bytes 2752520 | tf_op jit(solution)/shard_map/ppermute | solution.py:801
  191.9 9.8 %collective-permute-start.19 = (bf16[16,2816]{1,0:T(8,128)(2,1)S(1)}, bf16[16,2816]{1,0:T(8,128)(2,1)S(1)}, u32[]{:S(2)}, u32[]{:S(2)}) collective-permute-start(bf16[16,2816]{1,0:T(8,128)(2,1)S(1)} %add_convert_fusion.8), channel_id=1, source_target_pairs={{0,1},{1,0},{2,3},{3,2},{4,5},{5,4},{6,7},{7,6},{8,9},{9,8},{10,11... | collective-permute-start | bytes 270344 | tf_op jit(solution)/shard_map/ppermute | solution.py:990
  193.5 9.4 %collective-permute-start.22 = (bf16[32,2304]{1,0:T(8,128)(2,1)S(1)}, bf16[32,2304]{1,0:T(8,128)(2,1)S(1)}, u32[]{:S(2)}, u32[]{:S(2)}) collective-permute-start(bf16[32,2304]{1,0:T(8,128)(2,1)S(1)} %get-tuple-element.271), channel_id=1, source_target_pairs={{0,4},{1,5},{2,6},{3,7},{4,0},{5,1},{6,2},{7,3},{8,12},{9,13},{10,... | collective-permute-start | bytes 442376 | tf_op jit(solution)/shard_map/ppermute | solution.py:923
  194.0 14.8 %collective-permute-start.23 = (bf16[32,2304]{1,0:T(8,128)(2,1)S(1)}, bf16[32,2304]{1,0:T(8,128)(2,1)S(1)}, u32[]{:S(2)}, u32[]{:S(2)}) collective-permute-start(bf16[32,2304]{1,0:T(8,128)(2,1)S(1)} %get-tuple-element.270), channel_id=1, source_target_pairs={{0,8},{1,9},{2,10},{3,11},{4,12},{5,13},{6,14},{7,15},{8,0},{9,1},... | collective-permute-start | bytes 442376 | tf_op jit(solution)/shard_map/ppermute | solution.py:923
  197.7 4.0 %copy-start.3 = (bf16[16,32,896]{2,1,0:T(8,128)(2,1)S(1)}, bf16[16,32,896]{2,1,0:T(8,128)(2,1)}, u32[]{:S(2)}) copy-start(bf16[16,32,896]{2,1,0:T(8,128)(2,1)} %get-tuple-element.222) | copy-start | bytes 2752516
  197.7 11.0 %collective-permute-start.24 = (bf16[32,2304]{1,0:T(8,128)(2,1)S(1)}, bf16[32,2304]{1,0:T(8,128)(2,1)S(1)}, u32[]{:S(2)}, u32[]{:S(2)}) collective-permute-start(bf16[32,2304]{1,0:T(8,128)(2,1)S(1)} %get-tuple-element.269), channel_id=1, source_target_pairs={{0,12},{1,13},{2,14},{3,15},{4,8},{5,9},{6,10},{7,11},{8,4},{9,5},... | collective-permute-start | bytes 442376 | tf_op jit(solution)/shard_map/ppermute | solution.py:923
  201.7 1.2 copy-start.14
  202.0 8.5 %collective-permute-start.20 = (bf16[8,32,896]{2,1,0:T(8,128)(2,1)S(1)}, bf16[8,32,896]{2,1,0:T(8,128)(2,1)S(1)}, u32[]{:S(2)}, u32[]{:S(2)}) collective-permute-start(bf16[8,32,896]{2,1,0:T(8,128)(2,1)S(1)} %slice.78), channel_id=1, source_target_pairs={{0,1},{1,0},{2,3},{3,2},{4,5},{5,4},{6,7},{7,6},{8,9},{9,8},{10,11... | collective-permute-start | bytes 1376264 | tf_op jit(solution)/shard_map/ppermute | solution.py:923
  202.9 7.7 %collective-permute-start.25 = (bf16[4,208,512]{2,1,0:T(8,128)(2,1)S(1)}, bf16[4,208,512]{2,1,0:T(8,128)(2,1)S(1)}, u32[]{:S(2)}, u32[]{:S(2)}) collective-permute-start(bf16[4,208,512]{2,1,0:T(8,128)(2,1)S(1)} %copy-done.14), channel_id=1, source_target_pairs={{0,16},{16,0},{1,17},{17,1},{2,18},{18,2},{3,19},{19,3},{4,20},{20... | collective-permute-start | bytes 2555912 | tf_op jit(solution)/shard_map/ppermute | solution.py:801
  202.9 5.8 %collective-permute-start.21 = (bf16[16,2816]{1,0:T(8,128)(2,1)S(1)}, bf16[16,2816]{1,0:T(8,128)(2,1)S(1)}, u32[]{:S(2)}, u32[]{:S(2)}) collective-permute-start(bf16[16,2816]{1,0:T(8,128)(2,1)S(1)} %add_convert_fusion.7), channel_id=1, source_target_pairs={{0,2},{1,3},{2,0},{3,1},{4,6},{5,7},{6,4},{7,5},{8,10},{9,11},{10,... | collective-permute-start | bytes 270344 | tf_op jit(solution)/shard_map/ppermute | solution.py:990
  204.3 13.0 %copy-start = (f32[4,392,512]{2,1,0:T(8,128)S(1)}, f32[4,392,512]{2,1,0:T(8,128)}, u32[]{:S(2)}) copy-start(f32[4,392,512]{2,1,0:T(8,128)} %get-tuple-element.245) | copy-start | bytes 9633796
  207.9 8.7 %copy-start.13 = (bf16[4,208,512]{2,1,0:T(8,128)(2,1)S(1)}, bf16[4,208,512]{2,1,0:T(8,128)(2,1)}, u32[]{:S(2)}) copy-start(bf16[4,208,512]{2,1,0:T(8,128)(2,1)} %get-tuple-element.249) | copy-start | bytes 2555908
  210.6 6.1 %collective-permute-start.27 = (bf16[16,2816]{1,0:T(8,128)(2,1)S(1)}, bf16[16,2816]{1,0:T(8,128)(2,1)S(1)}, u32[]{:S(2)}, u32[]{:S(2)}) collective-permute-start(bf16[16,2816]{1,0:T(8,128)(2,1)S(1)} %add_convert_fusion.6), channel_id=1, source_target_pairs={{0,4},{1,5},{2,6},{3,7},{4,0},{5,1},{6,2},{7,3},{8,12},{9,13},{10,... | collective-permute-start | bytes 270344 | tf_op jit(solution)/shard_map/ppermute | solution.py:923
  211.6 10.4 %collective-permute-start.28 = (bf16[16,2816]{1,0:T(8,128)(2,1)S(1)}, bf16[16,2816]{1,0:T(8,128)(2,1)S(1)}, u32[]{:S(2)}, u32[]{:S(2)}) collective-permute-start(bf16[16,2816]{1,0:T(8,128)(2,1)S(1)} %add_convert_fusion.6), channel_id=1, source_target_pairs={{0,8},{1,9},{2,10},{3,11},{4,12},{5,13},{6,14},{7,15},{8,0},{9,1},... | collective-permute-start | bytes 270344 | tf_op jit(solution)/shard_map/ppermute | solution.py:923
  214.8 7.2 %collective-permute-start.29 = (bf16[16,2816]{1,0:T(8,128)(2,1)S(1)}, bf16[16,2816]{1,0:T(8,128)(2,1)S(1)}, u32[]{:S(2)}, u32[]{:S(2)}) collective-permute-start(bf16[16,2816]{1,0:T(8,128)(2,1)S(1)} %add_convert_fusion.6), channel_id=1, source_target_pairs={{0,12},{1,13},{2,14},{3,15},{4,8},{5,9},{6,10},{7,11},{8,4},{9,5},... | collective-permute-start | bytes 270344 | tf_op jit(solution)/shard_map/ppermute | solution.py:923
  215.2 6.8 %collective-permute-start.26 = (bf16[4,32,896]{2,1,0:T(8,128)(2,1)S(1)}, bf16[4,32,896]{2,1,0:T(8,128)(2,1)S(1)}, u32[]{:S(2)}, u32[]{:S(2)}) collective-permute-start(bf16[4,32,896]{2,1,0:T(8,128)(2,1)S(1)} %slice.84), channel_id=1, source_target_pairs={{0,2},{1,3},{2,0},{3,1},{4,6},{5,7},{6,4},{7,5},{8,10},{9,11},{10,... | collective-permute-start | bytes 688136 | tf_op jit(solution)/shard_map/ppermute | solution.py:923
  216.6 5.4 %collective-permute-start.31 = (bf16[4,208,512]{2,1,0:T(8,128)(2,1)S(1)}, bf16[4,208,512]{2,1,0:T(8,128)(2,1)S(1)}, u32[]{:S(2)}, u32[]{:S(2)}) collective-permute-start(bf16[4,208,512]{2,1,0:T(8,128)(2,1)S(1)} %copy-done.13), channel_id=1, source_target_pairs={{0,16},{16,0},{1,17},{17,1},{2,18},{18,2},{3,19},{19,3},{4,20},{20... | collective-permute-start | bytes 2555912 | tf_op jit(solution)/shard_map/ppermute | solution.py:801
  216.7 5.3 %collective-permute-start.30 = (bf16[32,2304]{1,0:T(8,128)(2,1)S(1)}, bf16[32,2304]{1,0:T(8,128)(2,1)S(1)}, u32[]{:S(2)}, u32[]{:S(2)}) collective-permute-start(bf16[32,2304]{1,0:T(8,128)(2,1)S(1)} %fusion.7), channel_id=1, source_target_pairs={{0,16},{16,0},{1,17},{17,1},{2,18},{18,2},{3,19},{19,3},{4,20},{20... | collective-permute-start | bytes 442376 | tf_op jit(solution)/shard_map/ppermute | solution.py:801
  219.3 7.5 %copy-start.2 = (bf16[4,392,512]{2,1,0:T(8,128)(2,1)S(1)}, bf16[4,392,512]{2,1,0:T(8,128)(2,1)}, u32[]{:S(2)}) copy-start(bf16[4,392,512]{2,1,0:T(8,128)(2,1)} %get-tuple-element.252) | copy-start | bytes 4816900
  222.3 14.3 %collective-permute-start.32 = (bf16[32,896]{1,0:T(8,128)(2,1)S(1)}, bf16[32,896]{1,0:T(8,128)(2,1)S(1)}, u32[]{:S(2)}, u32[]{:S(2)}) collective-permute-start(bf16[32,896]{1,0:T(8,128)(2,1)S(1)} %get-tuple-element.280), channel_id=1, source_target_pairs={{0,4},{1,5},{2,6},{3,7},{4,0},{5,1},{6,2},{7,3},{8,12},{9,13},{10,... | collective-permute-start | bytes 172040 | tf_op jit(solution)/shard_map/ppermute | solution.py:923
  224.1 12.5 %collective-permute-start.33 = (bf16[32,896]{1,0:T(8,128)(2,1)S(1)}, bf16[32,896]{1,0:T(8,128)(2,1)S(1)}, u32[]{:S(2)}, u32[]{:S(2)}) collective-permute-start(bf16[32,896]{1,0:T(8,128)(2,1)S(1)} %get-tuple-element.279), channel_id=1, source_target_pairs={{0,8},{1,9},{2,10},{3,11},{4,12},{5,13},{6,14},{7,15},{8,0},{9,1},... | collective-permute-start | bytes 172040 | tf_op jit(solution)/shard_map/ppermute | solution.py:923
  225.7 10.9 %collective-permute-start.34 = (bf16[32,896]{1,0:T(8,128)(2,1)S(1)}, bf16[32,896]{1,0:T(8,128)(2,1)S(1)}, u32[]{:S(2)}, u32[]{:S(2)}) collective-permute-start(bf16[32,896]{1,0:T(8,128)(2,1)S(1)} %get-tuple-element.278), channel_id=1, source_target_pairs={{0,12},{1,13},{2,14},{3,15},{4,8},{5,9},{6,10},{7,11},{8,4},{9,5},... | collective-permute-start | bytes 172040 | tf_op jit(solution)/shard_map/ppermute | solution.py:923
  237.3 1.2 collective-permute-start.35
